TPU v7x, 512 devices: a whole 4x8x8 slice. The times are simulated.
512 devices in a mesh: group: 64 (over y, z), head: 8 (over x, core).
Axes of the slice: x: 4, y: 8, z: 8, core: 2. Of those that a mesh axis runs over, the one named last changes fastest.
Arguments:
- queries: bfloat16 [1024, 8, 64, 128], P('group', None, 'head'), may hold values from -12 to 12
- fresh_kv: bfloat16 [1024, 8, 8, 2, 128], P('group', None, 'head'), may hold values from -4 to 4
- page_pool: bfloat16 [4096, 8, 2, 128, 128], P('group', 'head'), may hold values from -6 to 6
- context_len: int32 [1024], P('group'), may hold values from 1 to 1024, as said below
- page_holder: int32 [1024, 8], P('group'), may hold values from 0 to 63, as said below
- page_index: int32 [1024, 8], P('group'), may hold values from 0 to 63
- hot_owner: int32 [1], replicated, may hold values from 0 to 63
- hot_pages: int32 [32], replicated, may hold values from 0 to 63
Outputs:
- attended: bfloat16 [1024, 8, 64, 128], P('group', None, 'head')
Inputs may be any that keep to these rules, and one draw needn't show every extreme that they name: `context_len`: in each decode group of 16 requests one request has exactly 1024 tokens. `page_holder`: among the entries of one decode group's 16 requests each holder group is named at most 2 times; entries of pages past a request's context are not read.
All inputs are finite; a program needn't handle non-finite values.
Results may differ from a plain program's by a relative error of at most 0.02.
Values may be sent and summed in bfloat16 or wider, within the bound.
No kernel may reach another device: no remote copies, remote signals or barrier semaphores. Data moves between devices by JAX's collectives and lax.ppermute only.
A program may use at most 128 MiB of HBM per device.

v0:
```python
import math

import jax
import jax.numpy as jnp
from jax import lax
from jax.sharding import PartitionSpec as P

NEG_FILL = -1e30


def spread(value, axis, source):
    kept = jnp.where(lax.axis_index(axis) == source, value, 0).astype(value.dtype)
    return lax.psum(kept, axis)


def hot_partial(query_rows, hot_keys, hot_values, score_scale):
    scores = (
        jnp.einsum("rsxgd,pxtd->rsxgpt", query_rows, hot_keys, preferred_element_type=jnp.float32)
        * score_scale
    )
    row_max = jnp.max(scores, axis=(4, 5))
    exponent = jnp.exp(scores - row_max[:, :, :, :, None, None])
    weight_sum = jnp.sum(exponent, axis=(4, 5))
    weighted = jnp.einsum(
        "rsxgpt,pxtd->rsxgd",
        exponent.astype(jnp.bfloat16),
        hot_values,
        preferred_element_type=jnp.float32,
    )
    return (row_max, weight_sum, weighted)


def page_partial(query_rows, own_pages, usable, score_scale):
    scores = (
        jnp.einsum(
            "rsxgd,rpxtd->rsxgpt",
            query_rows,
            own_pages[:, :, :, 0],
            preferred_element_type=jnp.float32,
        )
        * score_scale
    )
    allowed = usable[:, None, None, None, :, :]
    masked = jnp.where(allowed, scores, NEG_FILL)
    row_max = jnp.max(masked, axis=(4, 5))
    exponent = jnp.where(allowed, jnp.exp(masked - row_max[:, :, :, :, None, None]), 0.0)
    weight_sum = jnp.sum(exponent, axis=(4, 5))
    weighted = jnp.einsum(
        "rsxgpt,rpxtd->rsxgd",
        exponent.astype(jnp.bfloat16),
        own_pages[:, :, :, 1],
        preferred_element_type=jnp.float32,
    )
    return (row_max, weight_sum, weighted)


def fresh_partial(query_rows, fresh_kv, score_scale):
    steps = query_rows.shape[1]
    scores = (
        jnp.einsum(
            "rsxgd,rkxd->rsxgk",
            query_rows,
            fresh_kv[:, :, :, 0],
            preferred_element_type=jnp.float32,
        )
        * score_scale
    )
    step_order = jnp.arange(steps, dtype=jnp.int32)
    allowed = (step_order[None, :] <= step_order[:, None])[None, :, None, None, :]
    masked = jnp.where(allowed, scores, NEG_FILL)
    row_max = jnp.max(masked, axis=4)
    exponent = jnp.where(allowed, jnp.exp(masked - row_max[..., None]), 0.0)
    weight_sum = jnp.sum(exponent, axis=4)
    weighted = jnp.einsum(
        "rsxgk,rkxd->rsxgd",
        exponent.astype(jnp.bfloat16),
        fresh_kv[:, :, :, 1],
        preferred_element_type=jnp.float32,
    )
    return (row_max, weight_sum, weighted)


def combine_partials(row_max, weight_sum, weighted, stack_axis):
    largest = jnp.max(row_max, axis=stack_axis, keepdims=True)
    factor = jnp.exp(row_max - largest)
    total_sum = jnp.sum(weight_sum * factor, axis=stack_axis)
    mixture = jnp.sum(weighted * factor[..., None], axis=stack_axis)
    return (jnp.squeeze(largest, stack_axis), total_sum, mixture)


def on_device(
    queries, fresh_kv, page_pool, context_len, page_holder, page_index, hot_owner, hot_pages
):
    requests, steps, local_heads, head_dim = queries.shape
    kv_local = fresh_kv.shape[2]
    per_kv = local_heads // kv_local
    page_len = page_pool.shape[3]
    max_pages = page_holder.shape[1]
    groups = lax.axis_size("group")
    capacity = max(2, (requests * max_pages + groups - 1) // groups)
    score_scale = 1.0 / math.sqrt(head_dim)
    query_rows = queries.reshape(requests, steps, kv_local, per_kv, head_dim)
    hot_local = jnp.take(page_pool, hot_pages, axis=0)
    hot_kv = spread(hot_local, "group", hot_owner[0])
    hot_keys = hot_kv[:, :, 0]
    hot_values = hot_kv[:, :, 1]
    block_size = math.gcd(requests, max(1, 512 // (steps * per_kv)))
    blocks = requests // block_size

    def hot_block(block_rows):
        return hot_partial(block_rows, hot_keys, hot_values, score_scale)

    def unblock(stacked):
        return stacked.reshape((requests,) + stacked.shape[2:])

    hot_parts = lax.map(
        hot_block, query_rows.reshape(blocks, block_size, steps, kv_local, per_kv, head_dim)
    )
    hot_parts = jax.tree.map(unblock, hot_parts)
    page_order = jnp.arange(max_pages, dtype=jnp.int32)
    token_order = jnp.arange(page_len, dtype=jnp.int32)
    page_count = (context_len + page_len - 1) // page_len
    live_pages = page_order[None, :] < page_count[:, None]
    filled = jnp.clip(context_len[:, None] - page_order[None, :] * page_len, 0, page_len)
    flat_holder = page_holder.reshape(-1)
    flat_live = live_pages.reshape(-1)
    member = (
        (flat_holder[:, None] == jnp.arange(groups, dtype=jnp.int32)[None, :]) & flat_live[:, None]
    ).astype(jnp.int32)
    earlier = jnp.cumsum(member, axis=0) - member
    slot_rank = jnp.sum(earlier * member, axis=1)
    slot_flat = flat_holder * capacity + slot_rank
    gather_slot = jnp.where(flat_live, slot_flat, 0)
    target = jnp.where(flat_live, slot_flat, groups * capacity)
    slot_ids = (
        jnp.zeros((groups * capacity,), jnp.int32)
        .at[target]
        .set(page_index.reshape(-1), mode="drop")
    )
    slot_info = slot_ids.reshape(groups, capacity, 1)
    asked_for = lax.all_to_all(slot_info, "group", split_axis=0, concat_axis=0, tiled=True)
    served = jnp.take(page_pool, asked_for[:, :, 0].reshape(-1), axis=0)
    arrived = lax.all_to_all(
        served.reshape(groups, capacity, kv_local, 2, page_len, head_dim),
        "group",
        split_axis=0,
        concat_axis=0,
        tiled=True,
    )
    own_pages = jnp.take(
        arrived.reshape(groups * capacity, kv_local, 2, page_len, head_dim), gather_slot, axis=0
    )
    own_pages = own_pages.reshape(requests, max_pages, kv_local, 2, page_len, head_dim)
    usable = token_order[None, None, :] < filled[:, :, None]
    private = page_partial(query_rows, own_pages, usable, score_scale)
    fresh_part = fresh_partial(query_rows, fresh_kv, score_scale)
    row_max, weight_sum, weighted = combine_partials(
        jnp.stack((hot_parts[0], private[0], fresh_part[0])),
        jnp.stack((hot_parts[1], private[1], fresh_part[1])),
        jnp.stack((hot_parts[2], private[2], fresh_part[2])),
        0,
    )
    attended = (weighted / weight_sum[..., None]).astype(jnp.bfloat16)
    return attended.reshape(requests, steps, local_heads, head_dim)


def solution(mesh):
    placed = (
        P("group", None, "head", None),
        P("group", None, "head", None, None),
        P("group", "head", None, None, None),
        P("group"),
        P("group", None),
        P("group", None),
        P(),
        P(),
    )
    return jax.shard_map(
        on_device,
        mesh=mesh,
        in_specs=placed,
        out_specs=P("group", None, "head", None),
        check_vma=False,
    )
```

profile of v0, /device:TPU:6, one launch (start us, length us, event | category | flops | bytes accessed | tf_op | source)
XLA Modules:
  0.0 502.7 jit_solution(4425286499713994639)
XLA Ops:
  6.5 0.8 copy.31
  7.3 0.1 reshape.561
  7.4 0.7 and_select_fusion
  8.1 0.1 iota_compare_fusion.2
  8.1 0.1 lt.118
  8.2 0.1 lt.116
  8.3 0.1 mul.98
  8.4 0.1 fusion.53
  8.5 0.2 reduce_window_sum.11
  8.7 0.2 select_reduce_fusion
  8.9 0.8 copy.33
  9.6 0.1 reshape.605
  9.7 1.0 scatter_custom_fusion
  10.7 0.1 reshape.563
  10.9 28.4 %all_to_all.10 = s32[64,2,1]{1,2,0:T(1,128)S(1)} all-to-all(s32[64,2,1]{1,2,0:T(1,128)S(1)} %bitcast.262), channel_id=1, replica_groups=mesh['group'=64,'head'=8] {'group'}, dimensions={0} | all-to-all | bytes 1024 | tf_op jit(solution)/shard_map/all_to_all | solution.py:141
  39.2 0.5 broadcast.338
  39.7 0.7 reduce.17
  40.5 0.1 reshape_squeeze.6
  40.6 0.1 copy.35
  40.7 0.1 copy.36
  40.8 8.7 %gather_fusion.1 = bf16[128,2,128,128]{3,2,1,0:T(8,128)(2,1)} fusion(bf16[64,2,128,128]{3,2,1,0:T(8,128)(2,1)} %bitcast.246, s32[1024]{0:T(1024)S(1)} %pad_clamp_fusion.1), kind=kCustom, calls=%fused_computation.1 | custom fusion | bytes 16777728 | tf_op jit(solution)/shard_map/jit(_take)/gather | solution.py:142
  49.5 7.4 %broadcast_select_fusion = bf16[64,2,1,2,128,128]{5,4,3,1,2,0:T(8,128)(2,1)} fusion(bf16[64,2,1,2,128,128]{5,4,3,1,2,0:T(8,128)(2,1)} %bitcast.244, pred[64,2]{1,0:T(8,128)(4,1)S(1)} %copy.36), kind=kLoop, calls=%fused_computation.22 | loop fusion | flops 4194304 | bytes 16777344 | tf_op jit(solution)/shard_map/jit(_take)/select_n | solution.py:142
  57.0 5.9 %all-to-all-start.1 = ((bf16[64,2,1,2,128,128]{5,4,3,1,2,0:T(8,128)(2,1)}), bf16[64,2,1,2,128,128]{5,4,3,1,2,0:T(8,128)(2,1)}, u32[]{:S(2)}, u32[]{:S(2)}) async-start(bf16[64,2,1,2,128,128]{5,4,3,1,2,0:T(8,128)(2,1)} %broadcast_select_fusion), calls=%async_computation.1 | async-start | bytes 16777216 | tf_op jit(solution)/shard_map/all_to_all | solution.py:143
  62.8 0.0 all-reduce.2.cloned.1.call-start
  62.9 3.1 gather_fusion
  66.1 0.0 copy-start.2
  66.1 0.0 copy-start.1
  66.8 0.0 copy-start.8
  66.8 1.6 fusion.27
  68.4 0.0 all-reduce.2.cloned.1.call-update
  68.5 0.1 reduce_sum.59
  68.5 0.6 copy.68
  69.2 0.6 pad_clamp_fusion
  69.8 0.1 fusion.63
  69.9 1.3 fusion.64
  71.2 0.9 fusion.40
  72.1 0.4 convolution_bitcast_fusion
  72.4 0.1 subtract_clamp_fusion
  72.5 0.7 compare_and_fusion
  73.2 0.1 iota_compare_fusion
  73.3 375.0 %all-reduce.2.cloned.1.call-done = bf16[32,1,2,128,128]{4,3,2,0,1:T(8,128)(2,1)} async-done(((bf16[32,1,2,128,128]{4,3,2,0,1:T(8,128)(2,1)}), bf16[32,1,2,128,128]{4,3,2,0,1:T(8,128)(2,1)}) %all-reduce.2.cloned.1.call-update) | async-done | bytes 2097168 | tf_op jit(solution)/shard_map/psum | solution.py:13
  448.3 1.7 slice_bitcast_fusion.6
  450.0 8.9 %while.14 = (s32[]{:T(128)}, f32[2,8,8,1,8]{4,2,1,3,0:T(8,128)S(1)}, f32[2,8,8,1,8]{4,3,2,1,0:T(1,128)}, f32[2,8,8,1,8,128]{5,4,2,1,3,0:T(8,128)S(1)}, bf16[2,8,...) while((s32[]{:T(128)}, ...), condition=%wide.region_4.5_spmd, body=%wide.region_1.4_spmd.sunk | while | flops 1090518016 | bytes 27859108 | solution.py:116
  450.2 1.3 bitcast_reduce_fusion.3
  451.6 0.0 copy-start.4
  451.6 1.5 fusion.72
  453.1 0.0 copy-start.5
  453.1 1.4 fusion.73
  454.6 1.3 bitcast_reduce_fusion.3
  455.9 0.0 copy-start.4
  455.9 1.5 fusion.72
  457.4 0.0 copy-start.5
  457.5 1.4 fusion.73
  458.9 9.9 %gather_fusion.2 = bf16[128,2,128,128]{3,2,1,0:T(8,128)(2,1)} fusion(bf16[128,2,128,128]{3,2,1,0:T(8,128)(2,1)} %bitcast.31, s32[1024]{0:T(1024)} %pad_clamp_fusion), kind=kCustom, calls=%fused_computation.2 | custom fusion | bytes 16777728 | tf_op jit(solution)/shard_map/jit(_take)/gather | solution.py:150
  468.9 10.3 %copy.38 = bf16[128,2,128,128]{3,2,0,1:T(8,128)(2,1)} copy(bf16[128,2,128,128]{3,2,1,0:T(8,128)(2,1)} %gather_fusion.2) | data formatting | bytes 16777216 | tf_op jit(solution)/shard_map/jit(_take)/gather | solution.py:150
  479.2 7.4 %broadcast_select_fusion.1 = bf16[16,8,1,2,128,128]{5,4,1,0,3,2:T(8,128)(2,1)} fusion(bf16[16,8,1,2,128,128]{5,4,1,0,3,2:T(8,128)(2,1)} %bitcast.245, pred[16,8]{1,0:T(8,128)(4,1)S(1)} %copy-done.7), kind=kLoop, calls=%fused_computation.23 | loop fusion | flops 4194304 | bytes 16777344 | tf_op jit(solution)/shard_map/jit(_take)/select_n | solution.py:150
  486.6 4.0 bitcast_reduce_fusion.1
  490.6 0.6 copy-done
  491.3 1.6 fusion.36
  492.9 0.0 copy-start.6
  492.9 1.4 fusion.23
  494.4 0.5 fusion.34
  494.9 0.1 fusion.49
  494.9 0.9 divide_convert_fusion
  (34 shorter events, 0.2 us)
Async XLA Ops:
  57.0 5.9 %copy-start.9 = (s32[32]{0:T(128)S(1)}, s32[32]{0:T(128)}, u32[]{:S(2)}) copy-start(s32[32]{0:T(128)} %param.17) | copy-start | bytes 388
  57.0 401.9 %all-to-all-start.1 = ((bf16[64,2,1,2,128,128]{5,4,3,1,2,0:T(8,128)(2,1)}), bf16[64,2,1,2,128,128]{5,4,3,1,2,0:T(8,128)(2,1)}, u32[]{:S(2)}, u32[]{:S(2)}) async-start(bf16[64,2,1,2,128,128]{5,4,3,1,2,0:T(8,128)(2,1)} %broadcast_select_fusion), calls=%async_computation.1 | async-start | bytes 16777216 | tf_op jit(solution)/shard_map/all_to_all | solution.py:143
  62.8 385.5 %all-reduce.2.cloned.1.call-start = ((), (), s32[]{:S(2)}) async-start(), calls=%async_computation.2 | async-start | bytes 4194304 | tf_op jit(solution)/shard_map/psum | solution.py:13
  66.1 3.7 copy-start.2
  66.1 3.8 copy-start.1
  66.8 5.6 %copy-start.8 = (s32[16]{0:T(128)S(1)}, s32[16]{0:T(128)}, u32[]{:S(2)}) copy-start(s32[16]{0:T(128)} %param.13) | copy-start | bytes 196
  451.6 1.5 copy-start.4
  453.1 1.4 copy-start.5
  455.9 1.5 copy-start.4
  457.4 1.4 copy-start.5
  468.9 10.3 %copy-start.7 = (pred[16,8]{1,0:T(8,128)(4,1)S(1)}, pred[16,8]{1,0:T(8,128)(4,1)}, u32[]{:S(2)}) copy-start(pred[16,8]{1,0:T(8,128)(4,1)} %compare_and_fusion) | copy-start | bytes 388
  486.6 4.6 copy-start
  492.8 2.0 copy-start.3
  492.9 2.0 copy-start.6
Sparse Core Ops, SparseCore 0:
  68.6 379.6 all-reduce.1
where the time goes:
time: 503 us
  waiting for transfers between devices  375 us (75%)
  local copies, waits for them, and re-layouts  39.3 us (8%)
  blocking collectives  28.4 us (6%)
  other arithmetic  26.6 us (5%)
  between operations  14.4 us (3%)
  matrix products  12.7 us (3%)
  starting transfers between devices  5.92 us (1%)
    psum x1, waiting for transfers between devices, spread(): return lax.psum(kept, axis)  375 us
    all_to_all x1, blocking collectives, on_device(): lax.all_to_all(slot_info, 'group', split_axis=0, concat_axis=0, tiled=True)  28.4 us
    gather x2, local copies, waits for them, and re-layouts, on_device(): jnp.take(arrived.reshape(groups * capacity, kv_local, 2, page_len, head_d...  20.3 us
  transfers between devices with their start and end apart: 2, of which 1 were waited for; matrix products, arithmetic and copies ran while one was open for 4% of the time, Pallas kernels for 0%

commit v1 on v0

v1 whole, which is shorter than its diff:
```python
import functools
import math

import jax
import jax.numpy as jnp
from jax import lax
from jax.experimental import pallas as pl
from jax.experimental.pallas import tpu as pltpu
from jax.sharding import PartitionSpec as P

NEG_FILL = -1e30
CAP = 2
EXTRA = 8
VMEM_LIMIT = 48 * 1024 * 1024

SMEM_SPEC = pl.BlockSpec(memory_space=pltpu.SMEM)
VMEM_SPEC = pl.BlockSpec(memory_space=pltpu.VMEM)


def spread(value, axis, source):
    kept = jnp.where(lax.axis_index(axis) == source, value, 0).astype(value.dtype)
    return lax.psum(kept, axis)


def ask_kernel(len_ref, holder_ref, index_ref, q_ref, ask_ref, slot_ref, count_ref, *, page_len):
    requests, max_pages = holder_ref.shape
    groups = ask_ref.shape[0]
    rows = q_ref.shape[1]
    body = CAP * rows
    lanes = ask_ref.shape[2]

    def clear(g, carry):
        count_ref[g] = 0
        ask_ref[g, pl.ds(body, EXTRA), :] = jnp.zeros((EXTRA, lanes), ask_ref.dtype)
        return carry

    lax.fori_loop(0, groups, clear, 0)
    sub = lax.broadcasted_iota(jnp.int32, (EXTRA, lanes), 0)
    lane = lax.broadcasted_iota(jnp.int32, (EXTRA, lanes), 1)

    def one(i, carry):
        r = i // max_pages
        p = i - r * max_pages
        filled = jnp.clip(len_ref[r] - p * page_len, 0, page_len)
        slot_ref[i] = -1

        @pl.when(filled > 0)
        def _():
            h = holder_ref[r, p]
            rank = jnp.minimum(count_ref[h], CAP - 1)
            count_ref[h] = rank + 1
            slot_ref[i] = h * CAP + rank
            ask_ref[h, pl.ds(pl.multiple_of(rank * rows, rows), rows), :] = q_ref[r]
            page = index_ref[r, p].astype(jnp.float32)
            old = ask_ref[h, pl.ds(body, EXTRA), :].astype(jnp.float32)
            new = jnp.where(lane == 0, page, filled.astype(jnp.float32))
            ask_ref[h, pl.ds(body, EXTRA), :] = jnp.where(
                (sub == rank) & (lane < 2), new, old
            ).astype(ask_ref.dtype)

        return carry

    lax.fori_loop(0, requests * max_pages, one, 0)


def ask(context_len, page_holder, page_index, q, groups, page_len):
    requests, max_pages = page_holder.shape
    rows, lanes = q.shape[1:]
    return pl.pallas_call(
        functools.partial(ask_kernel, page_len=page_len),
        out_shape=(
            jax.ShapeDtypeStruct((groups, CAP * rows + EXTRA, lanes), q.dtype),
            jax.ShapeDtypeStruct((requests * max_pages,), jnp.int32),
        ),
        in_specs=[SMEM_SPEC, SMEM_SPEC, SMEM_SPEC, VMEM_SPEC],
        out_specs=(VMEM_SPEC, SMEM_SPEC),
        scratch_shapes=[pltpu.SMEM((groups,), jnp.int32)],
        compiler_params=pltpu.CompilerParams(vmem_limit_bytes=VMEM_LIMIT),
    )(context_len, page_holder, page_index, q)


def serve_kernel(table_ref, asked_ref, pool_ref, out_ref, *, score_scale):
    block = asked_ref.shape[0]
    lanes = asked_ref.shape[2]
    body = asked_ref.shape[1] - EXTRA
    rows = body // CAP
    page_len = pool_ref.shape[2]
    step = pl.program_id(0)
    token = lax.broadcasted_iota(jnp.int32, (rows, page_len), 1)
    column = lax.broadcasted_iota(jnp.int32, (body, lanes), 1)
    scores = []
    pages = []
    for g in range(block):
        for s in range(CAP):
            at = ((step * block + g) * CAP + s) * 2
            page = jnp.clip(table_ref[at], 0, pool_ref.shape[0] - 1)
            filled = table_ref[at + 1]
            q = asked_ref[g, s * rows : (s + 1) * rows, :]
            keys = pool_ref[page, 0]
            sc = lax.dot_general(
                q, keys, (((1,), (1,)), ((), ())), preferred_element_type=jnp.float32
            )
            scores.append(jnp.where(token < filled, sc * score_scale, NEG_FILL))
            pages.append(page)
    stats = jnp.zeros((body, lanes), jnp.float32)
    for g in range(block):
        both = []
        for s in range(CAP):
            sc = scores[g * CAP + s]
            top = jnp.max(sc, axis=1, keepdims=True)
            ex = jnp.exp(sc - top)
            total = jnp.sum(ex, axis=1, keepdims=True)
            mix = jnp.dot(
                ex.astype(jnp.bfloat16),
                pool_ref[pages[g * CAP + s], 1],
                preferred_element_type=jnp.float32,
            )
            out_ref[g, s * rows : (s + 1) * rows, :] = (mix / total).astype(out_ref.dtype)
            both.append(top + jnp.log(total))
        stats = jnp.where(column == g, jnp.concatenate(both, axis=0), stats)
    flat = stats.T
    high = flat.astype(jnp.bfloat16).astype(jnp.float32)
    low = flat - high
    sub = lax.broadcasted_iota(jnp.int32, (EXTRA, lanes), 0)
    for g in range(block):
        tile = jnp.where(sub == 0, high[g : g + 1], jnp.where(sub == 1, low[g : g + 1], 0.0))
        out_ref[g, body : body + EXTRA, :] = tile.astype(out_ref.dtype)


def serve(table, asked, pool, score_scale, block=8):
    groups, tall, lanes = asked.shape
    n_pages, _, page_len, head_dim = pool.shape
    return pl.pallas_call(
        functools.partial(serve_kernel, score_scale=score_scale),
        out_shape=jax.ShapeDtypeStruct(asked.shape, asked.dtype),
        grid_spec=pltpu.PrefetchScalarGridSpec(
            num_scalar_prefetch=1,
            grid=(groups // block,),
            in_specs=[
                pl.BlockSpec((block, tall, lanes), lambda i, t: (i, 0, 0)),
                pl.BlockSpec((n_pages, 2, page_len, head_dim), lambda i, t: (0, 0, 0, 0)),
            ],
            out_specs=pl.BlockSpec((block, tall, lanes), lambda i, t: (i, 0, 0)),
        ),
        compiler_params=pltpu.CompilerParams(vmem_limit_bytes=VMEM_LIMIT),
    )(table, asked, pool)


def near_kernel(q_ref, fresh_ref, hot_ref, mix_ref, stat_ref, *, score_scale, per_kv, chunk):
    block, rows, lanes = q_ref.shape
    steps = fresh_ref.shape[2]
    tokens = hot_ref.shape[1]
    q = q_ref[...].reshape(block * rows, lanes)
    rhs_t = (((1,), (1,)), ((), ()))
    row_step = lax.broadcasted_iota(jnp.int32, (rows, steps), 0) // per_kv
    key_step = lax.broadcasted_iota(jnp.int32, (rows, steps), 1)
    fresh_scores = []
    for b in range(block):
        sc = lax.dot_general(
            q_ref[b], fresh_ref[b, 0], rhs_t, preferred_element_type=jnp.float32
        )
        fresh_scores.append(jnp.where(key_step <= row_step, sc * score_scale, NEG_FILL))
    fresh_all = jnp.concatenate(fresh_scores, axis=0)
    top = jnp.max(fresh_all, axis=1, keepdims=True)
    ex = jnp.exp(fresh_all - top)
    total = jnp.sum(ex, axis=1, keepdims=True)
    exb = ex.astype(jnp.bfloat16)
    mix = jnp.concatenate(
        [
            jnp.dot(
                exb[b * rows : (b + 1) * rows],
                fresh_ref[b, 1],
                preferred_element_type=jnp.float32,
            )
            for b in range(block)
        ],
        axis=0,
    )
    for c in range(tokens // chunk):
        at = slice(c * chunk, (c + 1) * chunk)
        sc = (
            lax.dot_general(q, hot_ref[0, at, :], rhs_t, preferred_element_type=jnp.float32)
            * score_scale
        )
        new_top = jnp.maximum(top, jnp.max(sc, axis=1, keepdims=True))
        ex = jnp.exp(sc - new_top)
        keep = jnp.exp(top - new_top)
        total = total * keep + jnp.sum(ex, axis=1, keepdims=True)
        mix = mix * keep + jnp.dot(
            ex.astype(jnp.bfloat16), hot_ref[1, at, :], preferred_element_type=jnp.float32
        )
        top = new_top
    mix_ref[...] = (mix / total).reshape(block, rows, lanes)
    lse = top + jnp.log(total)
    stat_ref[...] = jnp.broadcast_to(lse, (block * rows, lanes)).reshape(block, rows, lanes)


def near(q, fresh, hot, score_scale, per_kv, block=2, chunk=1024):
    requests, rows, lanes = q.shape
    steps = fresh.shape[2]
    tokens = hot.shape[1]
    spec = pl.BlockSpec((block, rows, lanes), lambda i: (i, 0, 0))
    return pl.pallas_call(
        functools.partial(near_kernel, score_scale=score_scale, per_kv=per_kv, chunk=chunk),
        out_shape=(
            jax.ShapeDtypeStruct(q.shape, jnp.float32),
            jax.ShapeDtypeStruct(q.shape, jnp.float32),
        ),
        grid=(requests // block,),
        in_specs=[
            spec,
            pl.BlockSpec((block, 2, steps, lanes), lambda i: (i, 0, 0, 0)),
            pl.BlockSpec((2, tokens, lanes), lambda i: (0, 0, 0)),
        ],
        out_specs=(spec, spec),
        compiler_params=pltpu.CompilerParams(vmem_limit_bytes=VMEM_LIMIT),
        cost_estimate=pl.CostEstimate(
            flops=4 * requests * rows * tokens * lanes,
            bytes_accessed=2 * tokens * lanes * 2,
            transcendentals=requests * rows * tokens,
        ),
    )(q, fresh, hot)


def merge_kernel(slot_ref, served_ref, mix_ref, stat_ref, out_ref, lse_ref, *, max_pages):
    groups = served_ref.shape[0]
    requests, rows, lanes = mix_ref.shape
    body = CAP * rows

    def unpack(g, carry):
        tile = served_ref[g, pl.ds(body, EXTRA), :].astype(jnp.float32)
        lse_ref[pl.ds(g, 1), :] = tile[0:1] + tile[1:2]
        return carry

    lax.fori_loop(0, groups, unpack, 0)
    lse_ref[pl.ds(body, body), :] = lse_ref[pl.ds(0, body), :].T
    column = lax.broadcasted_iota(jnp.int32, (rows, lanes), 1)

    def one(r, carry):
        own = stat_ref[r]
        own_top = jnp.max(own, axis=1, keepdims=True)
        tops = []
        for p in range(max_pages):
            slot = slot_ref[r * max_pages + p]
            safe = jnp.maximum(slot, 0)
            h = safe // CAP
            rank = safe - h * CAP
            picked = lse_ref[pl.ds(pl.multiple_of(body + rank * rows, rows), rows), :]
            lse = jnp.sum(jnp.where(column == h, picked, 0.0), axis=1, keepdims=True)
            tops.append(jnp.where(slot >= 0, lse, NEG_FILL))
        top = own_top
        for p in range(max_pages):
            top = jnp.maximum(top, tops[p])
        weight = jnp.exp(own_top - top)
        total = weight
        mix = mix_ref[r] * weight
        for p in range(max_pages):
            slot = slot_ref[r * max_pages + p]
            safe = jnp.maximum(slot, 0)
            h = safe // CAP
            rank = safe - h * CAP
            weight = jnp.exp(tops[p] - top)
            total = total + weight
            part = served_ref[h, pl.ds(pl.multiple_of(rank * rows, rows), rows), :]
            mix = mix + jnp.where(slot >= 0, part.astype(jnp.float32) * weight, 0.0)
        out_ref[r] = (mix / total).astype(out_ref.dtype)
        return carry

    lax.fori_loop(0, requests, one, 0)


def merge(slots, served, mix, stat, max_pages):
    requests, rows, lanes = mix.shape
    return pl.pallas_call(
        functools.partial(merge_kernel, max_pages=max_pages),
        out_shape=jax.ShapeDtypeStruct(mix.shape, jnp.bfloat16),
        in_specs=[SMEM_SPEC, VMEM_SPEC, VMEM_SPEC, VMEM_SPEC],
        out_specs=VMEM_SPEC,
        scratch_shapes=[pltpu.VMEM((2 * CAP * rows, lanes), jnp.float32)],
        compiler_params=pltpu.CompilerParams(vmem_limit_bytes=VMEM_LIMIT),
    )(slots, served, mix, stat)


def on_device(
    queries, fresh_kv, page_pool, context_len, page_holder, page_index, hot_owner, hot_pages
):
    requests, steps, local_heads, head_dim = queries.shape
    page_len = page_pool.shape[3]
    max_pages = page_holder.shape[1]
    groups = lax.axis_size("group")
    score_scale = 1.0 / math.sqrt(head_dim)
    q = queries.reshape(requests, steps * local_heads, head_dim)
    fresh = fresh_kv[:, :, 0].transpose(0, 2, 1, 3)
    pool = page_pool[:, 0]
    hot_local = jnp.take(pool, hot_pages, axis=0, mode="clip")
    hot = spread(hot_local, "group", hot_owner[0])
    hot = hot.transpose(1, 0, 2, 3).reshape(2, -1, head_dim)
    asked, slots = ask(context_len, page_holder, page_index, q, groups, page_len)
    asked = lax.all_to_all(asked, "group", split_axis=0, concat_axis=0, tiled=True)
    body = CAP * steps * local_heads
    table = asked[:, body : body + CAP, 0:2].astype(jnp.int32).reshape(-1)
    served = serve(table, asked, pool, score_scale)
    served = lax.all_to_all(served, "group", split_axis=0, concat_axis=0, tiled=True)
    mix, stat = near(q, fresh, hot, score_scale, local_heads)
    attended = merge(slots, served, mix, stat, max_pages)
    return attended.reshape(requests, steps, local_heads, head_dim)


def solution(mesh):
    placed = (
        P("group", None, "head", None),
        P("group", None, "head", None, None),
        P("group", "head", None, None, None),
        P("group"),
        P("group", None),
        P("group", None),
        P(),
        P(),
    )
    return jax.shard_map(
        on_device,
        mesh=mesh,
        in_specs=placed,
        out_specs=P("group", None, "head", None),
        check_vma=False,
    )
```

time: 503 us -> 338 us (0.67)
  waiting for transfers between devices: 375 us -> 187 us
  blocking collectives: 28.4 us -> 75.5 us
  Pallas kernels: 0 us -> 38.1 us
  other arithmetic: 26.6 us -> 0.18 us
  local copies, waits for them, and re-layouts: 39.3 us -> 14.3 us
  matrix products: 12.7 us -> 0 us
    psum x1, waiting for transfers between devices: 375 us -> 187 us  [spread(): return lax.psum(kept, axis)]
    all_to_all x1, blocking collectives: 28.4 us -> 75.5 us  [on_device(): lax.all_to_all(asked, 'group', split_axis=0, concat_axis=0, tiled=True)]
    pallas_call x0 -> x4, Pallas kernels: none -> 38.1 us  [the longest x1 14.7 us: near(): pl.pallas_call(functools.partial(near_kernel, score_scale=score_scale, pe...]
    gather x4 -> x1, local copies, waits for them, and re-layouts: 32.1 us -> 4.32 us  [on_device(): hot_local = jnp.take(pool, hot_pages, axis=0, mode='clip')]
    select_n x7 -> x0, other arithmetic: 17.1 us -> none  [the longest x2 7.42 us: on_device(): jnp.take(arrived.reshape(groups * capacity, kv_local, 2, page_len, head_d...]
    dot_general x8 -> x0, matrix products: 12.7 us -> none  [the longest x1 3.99 us: page_partial(): jnp.einsum('rsxgd,rpxtd->rsxgpt', query_rows, own_pages[:, :, :, 0], pref...]
    reduce_sum x7 -> x0, other arithmetic: 6.04 us -> none  [the longest x2 3.01 us: hot_partial(): weight_sum = jnp.sum(exponent, axis=(4, 5))]
    unnamed x19, local copies, waits for them, and re-layouts: 2.84 us -> 8.38 us
  transfers between devices with their start and end apart: 2 -> 2, of which waited for: 1 -> 1; matrix products, arithmetic and copies ran while one was open for 4% -> 2% of each run, Pallas kernels for 0% -> 4%
where the time goes in v1:
time: 338 us; the launch traced here: 337 us
  waiting for transfers between devices  187 us (55%)
  blocking collectives  75.5 us (22%)
  Pallas kernels  38.1 us (11%)
  local copies, waits for them, and re-layouts  14.3 us (4%)
  between operations  14.1 us (4%)
  starting transfers between devices  8.04 us (2%)
    psum x1, waiting for transfers between devices, spread(): return lax.psum(kept, axis)  187 us
    all_to_all x1, blocking collectives, on_device(): lax.all_to_all(asked, 'group', split_axis=0, concat_axis=0, tiled=True)  75.5 us
    pallas_call x1, Pallas kernels, near(): pl.pallas_call(functools.partial(near_kernel, score_scale=score_scale, pe...  14.7 us
    pallas_call x1, Pallas kernels, serve(): pl.pallas_call(functools.partial(serve_kernel, score_scale=score_scale),...  12.1 us
    unnamed x19, local copies, waits for them, and re-layouts  8.38 us
    all_to_all x1, starting transfers between devices, on_device(): lax.all_to_all(served, 'group', split_axis=0, concat_axis=0, tiled=True)  8 us
  transfers between devices with their start and end apart: 2, of which 1 were waited for; matrix products, arithmetic and copies ran while one was open for 2% of the time, Pallas kernels for 4%

profile of v1, /device:TPU:6, one launch (start us, length us, event | category | flops | bytes accessed | tf_op | source)
XLA Modules:
  0.0 337.4 jit_solution(14603720418415693566)
XLA Ops:
  6.5 0.8 copy.13.holder_ref
  7.3 0.8 copy.14.index_ref
  8.0 0.0 copy-start.1
  8.1 0.9 copy-done.1
  9.0 0.0 copy-start.4
  9.0 0.7 copy-done.4
  9.7 5.8 %shard_map.82 = (bf16[64,136,128]{2,1,0:T(8,128)(2,1)S(1)}, s32[128]{0:T(128)S(1)}) custom-call(s32[16]{0:T(128)S(1)} %copy-done.4, s32[16,8]{1,0:T(8,128)S(1)} %copy.13.holder_ref, s32[16,8]{1,0:T(8,128)S(1)} %copy.14.index_ref, bf16[16,64,128]{2,1,0:T(8,128)(2,1)S(1)} %bitcast.13), custom_call_target="tpu_custom_call" | custom-call | tf_op jit(solution)/shard_map/pallas_call | solution.py:69
  15.5 75.5 %all_to_all.10.asked_ref = bf16[64,136,128]{2,1,0:T(8,128)(2,1)S(1)} all-to-all(bf16[64,136,128]{2,1,0:T(8,128)(2,1)S(1)} %get-tuple-element.10), channel_id=1, replica_groups=mesh['group'=64,'head'=8] {'group'}, dimensions={0} | all-to-all | bytes 4456448 | tf_op jit(solution)/shard_map/all_to_all | solution.py:299
  91.0 0.1 reshape.20.table_ref
  91.1 12.1 %shard_map.83 = bf16[64,136,128]{2,1,0:T(8,128)(2,1)S(1)} custom-call(s32[256]{0:T(256)S(1)} %reshape.20.table_ref, bf16[64,136,128]{2,1,0:T(8,128)(2,1)S(1)} %all_to_all.10.asked_ref, bf16[64,2,128,128]{3,2,1,0:T(8,128)(2,1)} %bitcast.16), custom_call_target="tpu_custom_call" | custom-call | tf_op jit(solution)/shard_map/pallas_call | solution.py:133
  103.2 0.0 copy-start
  103.2 1.4 copy-done
  104.6 0.0 copy-start.7
  104.6 8.0 %all-to-all-start.1 = ((bf16[64,136,128]{2,1,0:T(8,128)(2,1)}), bf16[64,136,128]{2,1,0:T(8,128)(2,1)S(1)}, u32[]{:S(2)}, u32[]{:S(2)}) async-start(bf16[64,136,128]{2,1,0:T(8,128)(2,1)} %copy-done), calls=%async_computation.1 | async-start | bytes 4456448 | tf_op jit(solution)/shard_map/all_to_all | solution.py:303
  112.6 0.0 all-reduce.2.cloned.1.call-start
  113.3 0.0 copy-done.7
  113.3 4.3 %gather_fusion = bf16[32,2,128,128]{3,2,1,0:T(8,128)(2,1)} fusion(bf16[64,2,128,128]{3,2,1,0:T(8,128)(2,1)} %bitcast.17, s32[1024]{0:T(1024)S(1)} %pad_clamp_fusion), kind=kCustom, calls=%fused_computation | custom fusion | bytes 4194432 | tf_op jit(solution)/shard_map/jit(_take)/gather | solution.py:295
  117.7 0.1 select_bitcast_fusion
  117.8 1.5 copy.16
  119.3 0.0 copy-start.6
  119.3 0.0 copy-start.2
  119.3 0.0 all-reduce.2.cloned.1.call-update
  119.3 0.8 copy-done.6
  120.1 0.6 copy.18
  120.8 187.2 %all-reduce.2.cloned.1.call-done.hot_ref = bf16[2,4096,128]{2,1,0:T(8,128)(2,1)} async-done(((bf16[2,4096,128]{2,1,0:T(8,128)(2,1)}), bf16[2,4096,128]{2,1,0:T(8,128)(2,1)}) %all-reduce.2.cloned.1.call-update) | async-done | bytes 2097168 | tf_op jit(solution)/shard_map/psum | solution.py:22
  307.9 0.0 copy-done.2
  307.9 0.0 copy-start.3
  307.9 0.8 copy-done.3
  308.8 0.0 copy-start.5
  308.8 1.6 copy-done.5
  310.4 14.7 %shard_map.84 = (f32[16,64,128]{2,1,0:T(8,128)S(1)}, f32[16,64,128]{2,1,0:T(8,128)S(1)}) custom-call(bf16[16,64,128]{2,1,0:T(8,128)(2,1)S(1)} %bitcast.14, bf16[16,2,8,128]{3,2,1,0:T(8,128)(2,1)S(1)} %bitcast.15, bf16[2,4096,128]{2,1,0:T(8,128)(2,1)S(1)} %copy-done.5), custom_call_target="tpu_custom_call" | custom-call | flops 2147483648 | bytes 2097152 | tf_op jit(solution)/shard_map/pallas_call | solution.py:203
  325.1 0.0 all-to-all-done.1.served_ref
  325.1 5.5 %shard_map.85 = bf16[16,64,128]{2,1,0:T(8,128)(2,1)} custom-call(s32[128]{0:T(128)S(1)} %get-tuple-element.9.slot_ref, bf16[64,136,128]{2,1,0:T(8,128)(2,1)S(1)} %all-to-all-done.1.served_ref, f32[16,64,128]{2,1,0:T(8,128)S(1)} %get-tuple-element.11.mix_ref, f32[16,64,128]{2,1,0:T(8,128)S(1)} %get-tuple-element.12.stat_ref), custom_call_target="tpu_custom_call" | custom-call | tf_op jit(solution)/shard_map/pallas_call | solution.py:274
  (2 shorter events, 0.0 us)
Async XLA Ops:
  8.0 0.9 copy-start.1
  9.0 0.7 copy-start.4
  103.2 1.4 copy-start
  104.6 8.7 %copy-start.7 = (s32[32]{0:T(128)S(1)}, s32[32]{0:T(128)}, u32[]{:S(2)}) copy-start(s32[32]{0:T(128)} %param.15) | copy-start | bytes 388
  104.6 220.5 %all-to-all-start.1 = ((bf16[64,136,128]{2,1,0:T(8,128)(2,1)}), bf16[64,136,128]{2,1,0:T(8,128)(2,1)S(1)}, u32[]{:S(2)}, u32[]{:S(2)}) async-start(bf16[64,136,128]{2,1,0:T(8,128)(2,1)} %copy-done), calls=%async_computation.1 | async-start | bytes 4456448 | tf_op jit(solution)/shard_map/all_to_all | solution.py:303
  112.6 195.3 %all-reduce.2.cloned.1.call-start = ((), (), s32[]{:S(2)}) async-start(), calls=%async_computation.2 | async-start | bytes 4194304 | tf_op jit(solution)/shard_map/psum | solution.py:22
  119.3 0.8 copy-start.6
  119.3 188.6 %copy-start.2 = (bf16[16,8,8,128]{3,2,1,0:T(8,128)(2,1)S(1)}, bf16[16,8,8,128]{3,2,1,0:T(8,128)(2,1)}, u32[]{:S(2)}) copy-start(bf16[16,8,8,128]{3,2,1,0:T(8,128)(2,1)} %param.8) | copy-start | bytes 786436
  307.9 0.8 copy-start.3
  308.8 1.6 copy-start.5
Sparse Core Ops, SparseCore 0:
  119.4 188.4 all-reduce.1

commit v2 on v1

--- a/solution.py
+++ b/solution.py
@@ -17,9 +17,38 @@
 VMEM_SPEC = pl.BlockSpec(memory_space=pltpu.VMEM)
 
 
-def spread(value, axis, source):
-    kept = jnp.where(lax.axis_index(axis) == source, value, 0).astype(value.dtype)
-    return lax.psum(kept, axis)
+def pick_kernel(owns_ref, pages_ref, pool_ref, out_ref):
+    chunks = out_ref.shape[0]
+    page_len = pool_ref.shape[2]
+    per_chunk = out_ref.shape[2] // page_len
+
+    @pl.when(owns_ref[0] != 0)
+    def _():
+        def one(c, carry):
+            for p in range(per_chunk):
+                page = jnp.clip(pages_ref[c * per_chunk + p], 0, pool_ref.shape[0] - 1)
+                out_ref[c, :, p * page_len : (p + 1) * page_len, :] = pool_ref[page]
+            return carry
+
+        lax.fori_loop(0, chunks, one, 0)
+
+    @pl.when(owns_ref[0] == 0)
+    def _():
+        out_ref[...] = jnp.full(out_ref.shape, -jnp.inf, out_ref.dtype)
+
+
+def pick(owns, hot_pages, pool, chunks):
+    n_hot = hot_pages.shape[0]
+    _, two, page_len, head_dim = pool.shape
+    return pl.pallas_call(
+        pick_kernel,
+        out_shape=jax.ShapeDtypeStruct(
+            (chunks, two, n_hot // chunks * page_len, head_dim), pool.dtype
+        ),
+        in_specs=[SMEM_SPEC, SMEM_SPEC, VMEM_SPEC],
+        out_specs=VMEM_SPEC,
+        compiler_params=pltpu.CompilerParams(vmem_limit_bytes=VMEM_LIMIT),
+    )(owns, hot_pages, pool)
 
 
 def ask_kernel(len_ref, holder_ref, index_ref, q_ref, ask_ref, slot_ref, count_ref, *, page_len):
@@ -146,10 +175,10 @@
     )(table, asked, pool)
 
 
-def near_kernel(q_ref, fresh_ref, hot_ref, mix_ref, stat_ref, *, score_scale, per_kv, chunk):
+def near_kernel(q_ref, fresh_ref, hot_ref, mix_ref, stat_ref, *, score_scale, per_kv):
     block, rows, lanes = q_ref.shape
     steps = fresh_ref.shape[2]
-    tokens = hot_ref.shape[1]
+    chunks = hot_ref.shape[0]
     q = q_ref[...].reshape(block * rows, lanes)
     rhs_t = (((1,), (1,)), ((), ()))
     row_step = lax.broadcasted_iota(jnp.int32, (rows, steps), 0) // per_kv
@@ -176,10 +205,9 @@
         ],
         axis=0,
     )
-    for c in range(tokens // chunk):
-        at = slice(c * chunk, (c + 1) * chunk)
+    for c in range(chunks):
         sc = (
-            lax.dot_general(q, hot_ref[0, at, :], rhs_t, preferred_element_type=jnp.float32)
+            lax.dot_general(q, hot_ref[c, 0], rhs_t, preferred_element_type=jnp.float32)
             * score_scale
         )
         new_top = jnp.maximum(top, jnp.max(sc, axis=1, keepdims=True))
@@ -187,7 +215,7 @@
         keep = jnp.exp(top - new_top)
         total = total * keep + jnp.sum(ex, axis=1, keepdims=True)
         mix = mix * keep + jnp.dot(
-            ex.astype(jnp.bfloat16), hot_ref[1, at, :], preferred_element_type=jnp.float32
+            ex.astype(jnp.bfloat16), hot_ref[c, 1], preferred_element_type=jnp.float32
         )
         top = new_top
     mix_ref[...] = (mix / total).reshape(block, rows, lanes)
@@ -195,13 +223,14 @@
     stat_ref[...] = jnp.broadcast_to(lse, (block * rows, lanes)).reshape(block, rows, lanes)
 
 
-def near(q, fresh, hot, score_scale, per_kv, block=2, chunk=1024):
+def near(q, fresh, hot, score_scale, per_kv, block=2):
     requests, rows, lanes = q.shape
     steps = fresh.shape[2]
-    tokens = hot.shape[1]
+    chunks, _, chunk, _ = hot.shape
+    tokens = chunks * chunk
     spec = pl.BlockSpec((block, rows, lanes), lambda i: (i, 0, 0))
     return pl.pallas_call(
-        functools.partial(near_kernel, score_scale=score_scale, per_kv=per_kv, chunk=chunk),
+        functools.partial(near_kernel, score_scale=score_scale, per_kv=per_kv),
         out_shape=(
             jax.ShapeDtypeStruct(q.shape, jnp.float32),
             jax.ShapeDtypeStruct(q.shape, jnp.float32),
@@ -210,7 +239,7 @@
         in_specs=[
             spec,
             pl.BlockSpec((block, 2, steps, lanes), lambda i: (i, 0, 0, 0)),
-            pl.BlockSpec((2, tokens, lanes), lambda i: (0, 0, 0)),
+            pl.BlockSpec((chunks, 2, chunk, lanes), lambda i: (0, 0, 0, 0)),
         ],
         out_specs=(spec, spec),
         compiler_params=pltpu.CompilerParams(vmem_limit_bytes=VMEM_LIMIT),
@@ -292,9 +321,10 @@
     q = queries.reshape(requests, steps * local_heads, head_dim)
     fresh = fresh_kv[:, :, 0].transpose(0, 2, 1, 3)
     pool = page_pool[:, 0]
-    hot_local = jnp.take(pool, hot_pages, axis=0, mode="clip")
-    hot = spread(hot_local, "group", hot_owner[0])
-    hot = hot.transpose(1, 0, 2, 3).reshape(2, -1, head_dim)
+    owns = (hot_owner == lax.axis_index("group")).astype(jnp.int32)
+    kept = pick(owns, hot_pages, pool, 4)
+    q, kept = lax.optimization_barrier((q, kept))
+    hot = lax.pmax(kept, "group")
     asked, slots = ask(context_len, page_holder, page_index, q, groups, page_len)
     asked = lax.all_to_all(asked, "group", split_axis=0, concat_axis=0, tiled=True)
     body = CAP * steps * local_heads

time: 338 us -> 340 us (level)
  waiting for transfers between devices: 187 us -> 194 us
  local copies, waits for them, and re-layouts: 14.3 us -> 8.07 us
    pmax x0 -> x1, waiting for transfers between devices: none -> 193 us  [on_device(): hot = lax.pmax(kept, 'group')]
    psum x1 -> x0, waiting for transfers between devices: 187 us -> none  [spread(): return lax.psum(kept, axis)]
    gather x1 -> x0, local copies, waits for them, and re-layouts: 4.32 us -> none  [on_device(): hot_local = jnp.take(pool, hot_pages, axis=0, mode='clip')]
  transfers between devices with their start and end apart: 2 -> 2, of which waited for: 1 -> 1; matrix products, arithmetic and copies ran while one was open for 2% -> 0% of each run, Pallas kernels for 4% -> 4%
where the time goes in v2:
time: 340 us
  waiting for transfers between devices  194 us (57%)
  blocking collectives  75.1 us (22%)
  Pallas kernels  40.5 us (12%)
  between operations  14.1 us (4%)
  local copies, waits for them, and re-layouts  8.07 us (2%)
  starting transfers between devices  8.05 us (2%)
    pmax x1, waiting for transfers between devices, on_device(): hot = lax.pmax(kept, 'group')  193 us
    all_to_all x1, blocking collectives, on_device(): lax.all_to_all(asked, 'group', split_axis=0, concat_axis=0, tiled=True)  75.1 us
    pallas_call x1, Pallas kernels, near(): pl.pallas_call(functools.partial(near_kernel, score_scale=score_scale, pe...  14.4 us
    pallas_call x1, Pallas kernels, serve(): pl.pallas_call(functools.partial(serve_kernel, score_scale=score_scale),...  12.1 us
    all_to_all x1, starting transfers between devices, on_device(): lax.all_to_all(served, 'group', split_axis=0, concat_axis=0, tiled=True)  8 us
    unnamed x19, local copies, waits for them, and re-layouts  7.92 us
  transfers between devices with their start and end apart: 2, of which 1 were waited for; matrix products, arithmetic and copies ran while one was open for 0% of the time, Pallas kernels for 4%

profile of v2, /device:TPU:6, one launch (start us, length us, event | category | flops | bytes accessed | tf_op | source)
XLA Modules:
  0.0 340.0 jit_solution(10318126771154812067)
XLA Ops:
  7.2 0.8 copy.12.holder_ref
  7.9 0.8 copy.13.index_ref
  8.7 0.0 copy-start.5
  8.7 0.7 copy-done.5
  9.4 0.0 copy-start.2
  9.4 0.0 copy-start.4
  9.4 2.5 shard_map.82
  11.9 0.0 copy-start.1
  11.9 1.3 copy-done.1
  13.2 0.0 copy-done.2
  13.2 0.0 copy-done.4
  13.2 5.9 %shard_map.83 = (bf16[64,136,128]{2,1,0:T(8,128)(2,1)S(1)}, s32[128]{0:T(128)S(1)}) custom-call(s32[16]{0:T(128)S(1)} %copy-done.4, s32[16,8]{1,0:T(8,128)S(1)} %copy.12.holder_ref, s32[16,8]{1,0:T(8,128)S(1)} %copy.13.index_ref, bf16[16,64,128]{2,1,0:T(8,128)(2,1)S(1)} %bitcast.9), custom_call_target="tpu_custom_call" | custom-call | tf_op jit(solution)/shard_map/pallas_call | solution.py:98
  19.2 75.1 %all_to_all.10.asked_ref = bf16[64,136,128]{2,1,0:T(8,128)(2,1)S(1)} all-to-all(bf16[64,136,128]{2,1,0:T(8,128)(2,1)S(1)} %get-tuple-element.13), channel_id=1, replica_groups=mesh['group'=64,'head'=8] {'group'}, dimensions={0} | all-to-all | bytes 4456448 | tf_op jit(solution)/shard_map/all_to_all | solution.py:329
  94.3 0.1 reshape.16.table_ref
  94.4 12.1 %shard_map.84 = bf16[64,136,128]{2,1,0:T(8,128)(2,1)S(1)} custom-call(s32[256]{0:T(256)S(1)} %reshape.16.table_ref, bf16[64,136,128]{2,1,0:T(8,128)(2,1)S(1)} %all_to_all.10.asked_ref, bf16[64,2,128,128]{3,2,1,0:T(8,128)(2,1)} %bitcast.13), custom_call_target="tpu_custom_call" | custom-call | tf_op jit(solution)/shard_map/pallas_call | solution.py:162
  106.5 0.0 copy-start
  106.5 1.4 copy-done
  107.9 0.0 copy-start.7
  107.9 8.0 %all-to-all-start.1 = ((bf16[64,136,128]{2,1,0:T(8,128)(2,1)}), bf16[64,136,128]{2,1,0:T(8,128)(2,1)S(1)}, u32[]{:S(2)}, u32[]{:S(2)}) async-start(bf16[64,136,128]{2,1,0:T(8,128)(2,1)} %copy-done), calls=%async_computation.1 | async-start | bytes 4456448 | tf_op jit(solution)/shard_map/all_to_all | solution.py:333
  115.9 0.0 all-reduce.2.cloned.1.call-start
  115.9 0.7 all-reduce.2.cloned.1.call-update
  116.6 0.0 copy-done.7
  116.6 0.6 copy.16
  117.3 193.5 %all-reduce.2.cloned.1.call-done.hot_ref = bf16[4,2,1024,128]{3,2,1,0:T(8,128)(2,1)} async-done(((bf16[4,2,1024,128]{3,2,1,0:T(8,128)(2,1)}), bf16[4,2,1024,128]{3,2,1,0:T(8,128)(2,1)}) %all-reduce.2.cloned.1.call-update) | async-done | bytes 2097168 | tf_op jit(solution)/shard_map/pmax | solution.py:327
  310.7 0.0 copy-start.3
  310.7 0.8 copy-done.3
  311.5 0.0 copy-start.6
  311.6 1.6 copy-done.6
  313.1 14.4 %shard_map.85 = (f32[16,64,128]{2,1,0:T(8,128)S(1)}, f32[16,64,128]{2,1,0:T(8,128)S(1)}) custom-call(bf16[16,64,128]{2,1,0:T(8,128)(2,1)S(1)} %bitcast.10, bf16[16,2,8,128]{3,2,1,0:T(8,128)(2,1)S(1)} %bitcast.11, bf16[4,2,1024,128]{3,2,1,0:T(8,128)(2,1)S(1)} %copy-done.6), custom_call_target="tpu_custom_call" | custom-call | flops 2147483648 | bytes 2097152 | tf_op jit(solution)/shard_map/pallas_call | solution.py:232
  327.6 0.0 all-to-all-done.1.served_ref
  327.6 5.5 %shard_map.86 = bf16[16,64,128]{2,1,0:T(8,128)(2,1)} custom-call(s32[128]{0:T(128)S(1)} %get-tuple-element.12.slot_ref, bf16[64,136,128]{2,1,0:T(8,128)(2,1)S(1)} %all-to-all-done.1.served_ref, f32[16,64,128]{2,1,0:T(8,128)S(1)} %get-tuple-element.15.mix_ref, f32[16,64,128]{2,1,0:T(8,128)S(1)} %get-tuple-element.16.stat_ref), custom_call_target="tpu_custom_call" | custom-call | tf_op jit(solution)/shard_map/pallas_call | solution.py:303
  (1 shorter events, 0.0 us)
Async XLA Ops:
  8.7 0.7 copy-start.5
  9.4 3.8 %copy-start.2 = (bf16[16,8,8,128]{3,2,1,0:T(8,128)(2,1)S(1)}, bf16[16,8,8,128]{3,2,1,0:T(8,128)(2,1)}, u32[]{:S(2)}) copy-start(bf16[16,8,8,128]{3,2,1,0:T(8,128)(2,1)} %param.8) | copy-start | bytes 786436
  9.4 3.8 %copy-start.4 = (s32[16]{0:T(128)S(1)}, s32[16]{0:T(128)}, u32[]{:S(2)}) copy-start(s32[16]{0:T(128)} %len_ref.1) | copy-start | bytes 196
  11.9 1.3 copy-start.1
  106.5 1.4 copy-start
  107.9 8.8 %copy-start.7 = (bf16[16,8,1,2,128]{4,3,2,1,0:T(2,128)(2,1)S(1)}, bf16[16,8,1,2,128]{4,3,2,1,0:T(2,128)(2,1)}, u32[]{:S(2)}) copy-start(bf16[16,8,1,2,128]{4,3,2,1,0:T(2,128)(2,1)} %param.9) | copy-start | bytes 196612
  107.9 219.7 %all-to-all-start.1 = ((bf16[64,136,128]{2,1,0:T(8,128)(2,1)}), bf16[64,136,128]{2,1,0:T(8,128)(2,1)S(1)}, u32[]{:S(2)}, u32[]{:S(2)}) async-start(bf16[64,136,128]{2,1,0:T(8,128)(2,1)} %copy-done), calls=%async_computation.1 | async-start | bytes 4456448 | tf_op jit(solution)/shard_map/all_to_all | solution.py:333
  115.9 194.8 %all-reduce.2.cloned.1.call-start = ((), (), s32[]{:S(2)}) async-start(), calls=%async_computation.2 | async-start | bytes 4194304 | tf_op jit(solution)/shard_map/pmax | solution.py:327
  310.7 0.8 copy-start.3
  311.5 1.6 copy-start.6
Sparse Core Ops, SparseCore 0:
  119.9 190.7 all-reduce.1

commit v3 on v1

--- a/solution.py
+++ b/solution.py
@@ -17,9 +17,34 @@
 VMEM_SPEC = pl.BlockSpec(memory_space=pltpu.VMEM)
 
 
-def spread(value, axis, source):
-    kept = jnp.where(lax.axis_index(axis) == source, value, 0).astype(value.dtype)
-    return lax.psum(kept, axis)
+def deal_kernel(hot_ref, pool_ref, out_ref):
+    groups, dealt, _ = out_ref.shape
+    page_len = pool_ref.shape[2]
+    share = dealt // 2
+    per_page = page_len // share
+
+    def one(i, carry):
+        page = jnp.clip(hot_ref[i], 0, pool_ref.shape[0] - 1)
+        for part in range(per_page):
+            for half in range(2):
+                out_ref[i * per_page + part, half * share : (half + 1) * share, :] = pool_ref[
+                    page, half, part * share : (part + 1) * share, :
+                ]
+        return carry
+
+    lax.fori_loop(0, hot_ref.shape[0], one, 0)
+
+
+def deal(hot_pages, pool, groups):
+    page_len, head_dim = pool.shape[2:]
+    dealt = 2 * page_len * hot_pages.shape[0] // groups
+    return pl.pallas_call(
+        deal_kernel,
+        out_shape=jax.ShapeDtypeStruct((groups, dealt, head_dim), pool.dtype),
+        in_specs=[SMEM_SPEC, VMEM_SPEC],
+        out_specs=VMEM_SPEC,
+        compiler_params=pltpu.CompilerParams(vmem_limit_bytes=VMEM_LIMIT),
+    )(hot_pages, pool)
 
 
 def ask_kernel(len_ref, holder_ref, index_ref, q_ref, ask_ref, slot_ref, count_ref, *, page_len):
@@ -82,7 +107,7 @@
 def serve_kernel(table_ref, asked_ref, pool_ref, out_ref, *, score_scale):
     block = asked_ref.shape[0]
     lanes = asked_ref.shape[2]
-    body = asked_ref.shape[1] - EXTRA
+    body = out_ref.shape[1] - EXTRA
     rows = body // CAP
     page_len = pool_ref.shape[2]
     step = pl.program_id(0)
@@ -127,12 +152,13 @@
         out_ref[g, body : body + EXTRA, :] = tile.astype(out_ref.dtype)
 
 
-def serve(table, asked, pool, score_scale, block=8):
+def serve(table, asked, pool, rows, score_scale, block=8):
     groups, tall, lanes = asked.shape
+    back = CAP * rows + EXTRA
     n_pages, _, page_len, head_dim = pool.shape
     return pl.pallas_call(
         functools.partial(serve_kernel, score_scale=score_scale),
-        out_shape=jax.ShapeDtypeStruct(asked.shape, asked.dtype),
+        out_shape=jax.ShapeDtypeStruct((groups, back, lanes), asked.dtype),
         grid_spec=pltpu.PrefetchScalarGridSpec(
             num_scalar_prefetch=1,
             grid=(groups // block,),
@@ -140,16 +166,28 @@
                 pl.BlockSpec((block, tall, lanes), lambda i, t: (i, 0, 0)),
                 pl.BlockSpec((n_pages, 2, page_len, head_dim), lambda i, t: (0, 0, 0, 0)),
             ],
-            out_specs=pl.BlockSpec((block, tall, lanes), lambda i, t: (i, 0, 0)),
+            out_specs=pl.BlockSpec((block, back, lanes), lambda i, t: (i, 0, 0)),
         ),
         compiler_params=pltpu.CompilerParams(vmem_limit_bytes=VMEM_LIMIT),
     )(table, asked, pool)
 
 
-def near_kernel(q_ref, fresh_ref, hot_ref, mix_ref, stat_ref, *, score_scale, per_kv, chunk):
+def near_kernel(q_ref, fresh_ref, hot_ref, mix_ref, stat_ref, kv_ref, *, score_scale, per_kv):
     block, rows, lanes = q_ref.shape
     steps = fresh_ref.shape[2]
-    tokens = hot_ref.shape[1]
+    shares, _, share, _ = hot_ref.shape
+    chunks, _, chunk, _ = kv_ref.shape
+    per_chunk = shares // chunks
+
+    @pl.when(pl.program_id(0) == 0)
+    def _():
+        def lay(c, carry):
+            for i in range(per_chunk):
+                kv_ref[c, :, i * share : (i + 1) * share, :] = hot_ref[c * per_chunk + i]
+            return carry
+
+        lax.fori_loop(0, chunks, lay, 0)
+
     q = q_ref[...].reshape(block * rows, lanes)
     rhs_t = (((1,), (1,)), ((), ()))
     row_step = lax.broadcasted_iota(jnp.int32, (rows, steps), 0) // per_kv
@@ -176,10 +214,9 @@
         ],
         axis=0,
     )
-    for c in range(tokens // chunk):
-        at = slice(c * chunk, (c + 1) * chunk)
+    for c in range(chunks):
         sc = (
-            lax.dot_general(q, hot_ref[0, at, :], rhs_t, preferred_element_type=jnp.float32)
+            lax.dot_general(q, kv_ref[c, 0], rhs_t, preferred_element_type=jnp.float32)
             * score_scale
         )
         new_top = jnp.maximum(top, jnp.max(sc, axis=1, keepdims=True))
@@ -187,7 +224,7 @@
         keep = jnp.exp(top - new_top)
         total = total * keep + jnp.sum(ex, axis=1, keepdims=True)
         mix = mix * keep + jnp.dot(
-            ex.astype(jnp.bfloat16), hot_ref[1, at, :], preferred_element_type=jnp.float32
+            ex.astype(jnp.bfloat16), kv_ref[c, 1], preferred_element_type=jnp.float32
         )
         top = new_top
     mix_ref[...] = (mix / total).reshape(block, rows, lanes)
@@ -195,13 +232,14 @@
     stat_ref[...] = jnp.broadcast_to(lse, (block * rows, lanes)).reshape(block, rows, lanes)
 
 
-def near(q, fresh, hot, score_scale, per_kv, block=2, chunk=1024):
+def near(q, fresh, hot, score_scale, per_kv, block=2, chunks=4):
     requests, rows, lanes = q.shape
     steps = fresh.shape[2]
-    tokens = hot.shape[1]
+    shares, _, share, _ = hot.shape
+    tokens = shares * share
     spec = pl.BlockSpec((block, rows, lanes), lambda i: (i, 0, 0))
     return pl.pallas_call(
-        functools.partial(near_kernel, score_scale=score_scale, per_kv=per_kv, chunk=chunk),
+        functools.partial(near_kernel, score_scale=score_scale, per_kv=per_kv),
         out_shape=(
             jax.ShapeDtypeStruct(q.shape, jnp.float32),
             jax.ShapeDtypeStruct(q.shape, jnp.float32),
@@ -210,9 +248,10 @@
         in_specs=[
             spec,
             pl.BlockSpec((block, 2, steps, lanes), lambda i: (i, 0, 0, 0)),
-            pl.BlockSpec((2, tokens, lanes), lambda i: (0, 0, 0)),
+            pl.BlockSpec((shares, 2, share, lanes), lambda i: (0, 0, 0, 0)),
         ],
         out_specs=(spec, spec),
+        scratch_shapes=[pltpu.VMEM((chunks, 2, tokens // chunks, lanes), hot.dtype)],
         compiler_params=pltpu.CompilerParams(vmem_limit_bytes=VMEM_LIMIT),
         cost_estimate=pl.CostEstimate(
             flops=4 * requests * rows * tokens * lanes,
@@ -281,26 +320,39 @@
     )(slots, served, mix, stat)
 
 
+def exchange(value):
+    return lax.all_to_all(value, "group", split_axis=0, concat_axis=0, tiled=True)
+
+
 def on_device(
     queries, fresh_kv, page_pool, context_len, page_holder, page_index, hot_owner, hot_pages
 ):
     requests, steps, local_heads, head_dim = queries.shape
-    page_len = page_pool.shape[3]
     max_pages = page_holder.shape[1]
     groups = lax.axis_size("group")
     score_scale = 1.0 / math.sqrt(head_dim)
     q = queries.reshape(requests, steps * local_heads, head_dim)
     fresh = fresh_kv[:, :, 0].transpose(0, 2, 1, 3)
     pool = page_pool[:, 0]
-    hot_local = jnp.take(pool, hot_pages, axis=0, mode="clip")
-    hot = spread(hot_local, "group", hot_owner[0])
-    hot = hot.transpose(1, 0, 2, 3).reshape(2, -1, head_dim)
-    asked, slots = ask(context_len, page_holder, page_index, q, groups, page_len)
-    asked = lax.all_to_all(asked, "group", split_axis=0, concat_axis=0, tiled=True)
-    body = CAP * steps * local_heads
+    rows = steps * local_heads
+    body = CAP * rows
+    rows = steps * local_heads
+    body = CAP * rows
+    dealt = exchange(deal(hot_pages, pool, groups))
+    asked, slots = ask(
+        context_len, page_holder, page_index, q, groups, page_pool.shape[3]
+    )
+    asked, dealt = lax.optimization_barrier((asked, dealt))
+    asked = exchange(asked)
+    share = lax.dynamic_index_in_dim(dealt, hot_owner[0], 0, keepdims=False)
+    share = jnp.broadcast_to(share, (groups,) + share.shape)
+    asked, share = lax.optimization_barrier((asked, share))
+    hot = exchange(share)
     table = asked[:, body : body + CAP, 0:2].astype(jnp.int32).reshape(-1)
-    served = serve(table, asked, pool, score_scale)
-    served = lax.all_to_all(served, "group", split_axis=0, concat_axis=0, tiled=True)
+    served = serve(table, asked, pool, rows, score_scale)
+    served, hot = lax.optimization_barrier((served, hot))
+    served = exchange(served)
+    hot = hot.reshape(groups, 2, -1, head_dim)
     mix, stat = near(q, fresh, hot, score_scale, local_heads)
     attended = merge(slots, served, mix, stat, max_pages)
     return attended.reshape(requests, steps, local_heads, head_dim)

time: 338 us -> 280 us (0.83); the launches traced: 337 us -> 275 us
  blocking collectives: 75.5 us -> 0 us
  starting transfers between devices: 8.04 us -> 52.6 us
  waiting for transfers between devices: 187 us -> 171 us
  between operations: 14.1 us -> 0.77 us
  local copies, waits for them, and re-layouts: 14.3 us -> 7.63 us
  Pallas kernels: 38.1 us -> 43.4 us
    psum x1 -> x0, waiting for transfers between devices: 187 us -> none  [spread(): return lax.psum(kept, axis)]
    all_to_all x1 -> x4, waiting for transfers between devices: 0.01 us -> 171 us  [exchange(): lax.all_to_all(value, 'group', split_axis=0, concat_axis=0, tiled=True)]
    all_to_all x1 -> x0, blocking collectives: 75.5 us -> none  [on_device(): lax.all_to_all(asked, 'group', split_axis=0, concat_axis=0, tiled=True)]
    all_to_all x1 -> x4, starting transfers between devices: 8 us -> 52.6 us  [exchange(): lax.all_to_all(value, 'group', split_axis=0, concat_axis=0, tiled=True)]
    gather x1 -> x0, local copies, waits for them, and re-layouts: 4.32 us -> none  [on_device(): hot_local = jnp.take(pool, hot_pages, axis=0, mode='clip')]
    pallas_call x0 -> x1, Pallas kernels: none -> 3.85 us  [deal(): pl.pallas_call(deal_kernel, out_shape=jax.ShapeDtypeStruct((groups, dealt...]
    unnamed x19 -> x21, local copies, waits for them, and re-layouts: 8.38 us -> 4.85 us
  transfers between devices with their start and end apart: 2 -> 4, of which waited for: 1 -> 4; matrix products, arithmetic and copies ran while one was open for 2% -> 0% of each run, Pallas kernels for 4% -> 12%
where the time goes in v3:
time: 280 us; the launch traced here: 275 us
  waiting for transfers between devices  171 us (61%)
  starting transfers between devices  52.6 us (19%)
  Pallas kernels  43.4 us (16%)
  local copies, waits for them, and re-layouts  7.63 us (3%)
    all_to_all x4, waiting for transfers between devices, exchange(): lax.all_to_all(value, 'group', split_axis=0, concat_axis=0, tiled=True)  171 us
    all_to_all x4, starting transfers between devices, exchange(): lax.all_to_all(value, 'group', split_axis=0, concat_axis=0, tiled=True)  52.6 us
    pallas_call x1, Pallas kernels, near(): pl.pallas_call(functools.partial(near_kernel, score_scale=score_scale, pe...  16.2 us
    pallas_call x1, Pallas kernels, serve(): pl.pallas_call(functools.partial(serve_kernel, score_scale=score_scale),...  12.1 us
    pallas_call x1, Pallas kernels, ask(): pl.pallas_call(functools.partial(ask_kernel, page_len=page_len), out_shap...  5.77 us
  transfers between devices with their start and end apart: 4, of which 4 were waited for; matrix products, arithmetic and copies ran while one was open for 0% of the time, Pallas kernels for 12%

profile of v3, /device:TPU:6, one launch (start us, length us, event | category | flops | bytes accessed | tf_op | source)
XLA Modules:
  0.0 275.2 jit_solution(4856026371860957811)
XLA Ops:
  0.0 0.0 copy-start.3
  0.0 0.7 copy-done.3
  0.7 3.8 %shard_map.83 = bf16[64,128,128]{2,1,0:T(8,128)(2,1)} custom-call(s32[32]{0:T(128)S(1)} %copy-done.3, bf16[64,2,128,128]{3,2,1,0:T(8,128)(2,1)} %bitcast.18), custom_call_target="tpu_custom_call" | custom-call | tf_op jit(solution)/shard_map/pallas_call | solution.py:41
  4.5 0.0 copy-start.7
  4.5 0.0 copy-start.8
  4.5 0.0 copy-start.2
  4.5 0.0 copy-start.4
  4.5 16.7 %all-to-all-start = ((bf16[64,128,128]{2,1,0:T(8,128)(2,1)}), bf16[64,128,128]{2,1,0:T(8,128)(2,1)S(1)}, u32[]{:S(2)}, u32[]{:S(2)}) async-start(bf16[64,128,128]{2,1,0:T(8,128)(2,1)} %shard_map.83), calls=%async_computation | async-start | bytes 4194304 | tf_op jit(solution)/shard_map/all_to_all | solution.py:324
  21.3 0.0 copy-done.7
  21.3 0.1 copy.12.holder_ref
  21.3 0.0 copy-done.8
  21.3 0.1 copy.13.index_ref
  21.4 0.0 copy-done.2
  21.4 0.0 copy-done.4
  21.4 5.8 %shard_map.82 = (bf16[64,136,128]{2,1,0:T(8,128)(2,1)S(1)}, s32[128]{0:T(128)S(1)}) custom-call(s32[16]{0:T(128)S(1)} %copy-done.4, s32[16,8]{1,0:T(8,128)S(1)} %copy.12.holder_ref, s32[16,8]{1,0:T(8,128)S(1)} %copy.13.index_ref, bf16[16,64,128]{2,1,0:T(8,128)(2,1)S(1)} %bitcast.15), custom_call_target="tpu_custom_call" | custom-call | tf_op jit(solution)/shard_map/pallas_call | solution.py:94
  27.2 0.0 copy-start.1
  27.2 1.4 copy-done.1
  28.6 44.6 %all-to-all-done = bf16[64,128,128]{2,1,0:T(8,128)(2,1)S(1)} async-done(((bf16[64,128,128]{2,1,0:T(8,128)(2,1)}), bf16[64,128,128]{2,1,0:T(8,128)(2,1)S(1)}, u32[]{:S(2)}, u32[]{:S(2)}) %all-to-all-start) | async-done | bytes 2097184 | tf_op jit(solution)/shard_map/all_to_all | solution.py:324
  73.2 0.0 copy-start.5
  73.2 1.3 copy-done.5
  74.5 11.3 %all-to-all-start.1 = ((bf16[64,136,128]{2,1,0:T(8,128)(2,1)}), bf16[64,136,128]{2,1,0:T(8,128)(2,1)S(1)}, u32[]{:S(2)}, u32[]{:S(2)}) async-start(bf16[64,136,128]{2,1,0:T(8,128)(2,1)} %copy-done.1), calls=%async_computation.1 | async-start | bytes 4456448 | tf_op jit(solution)/shard_map/all_to_all | solution.py:324
  86.4 0.8 dynamic-slice_bitcast_fusion
  87.2 51.9 %all-to-all-done.1.asked_ref = bf16[64,136,128]{2,1,0:T(8,128)(2,1)S(1)} async-done(((bf16[64,136,128]{2,1,0:T(8,128)(2,1)}), bf16[64,136,128]{2,1,0:T(8,128)(2,1)S(1)}, u32[]{:S(2)}, u32[]{:S(2)}) %all-to-all-start.1) | async-done | bytes 2228256 | tf_op jit(solution)/shard_map/all_to_all | solution.py:324
  139.1 1.9 broadcast_in_dim.3
  140.9 14.0 %all-to-all-start.2 = ((bf16[64,128,128]{2,1,0:T(8,128)(2,1)}), bf16[64,128,128]{2,1,0:T(8,128)(2,1)}, u32[]{:S(2)}, u32[]{:S(2)}) async-start(bf16[64,128,128]{2,1,0:T(8,128)(2,1)} %broadcast_in_dim.3), calls=%async_computation.2 | async-start | bytes 4194304 | tf_op jit(solution)/shard_map/all_to_all | solution.py:324
  155.0 0.1 reshape.20.table_ref
  155.2 12.1 %shard_map.84 = bf16[64,136,128]{2,1,0:T(8,128)(2,1)S(1)} custom-call(s32[256]{0:T(256)S(1)} %reshape.20.table_ref, bf16[64,136,128]{2,1,0:T(8,128)(2,1)S(1)} %all-to-all-done.1.asked_ref, bf16[64,2,128,128]{3,2,1,0:T(8,128)(2,1)} %bitcast.19), custom_call_target="tpu_custom_call" | custom-call | tf_op jit(solution)/shard_map/pallas_call | solution.py:159
  167.2 0.0 copy-start
  167.2 1.4 copy-done
  168.6 0.0 copy-start.6
  168.6 36.7 %all-to-all-done.2 = bf16[64,128,128]{2,1,0:T(8,128)(2,1)} async-done(((bf16[64,128,128]{2,1,0:T(8,128)(2,1)}), bf16[64,128,128]{2,1,0:T(8,128)(2,1)}, u32[]{:S(2)}, u32[]{:S(2)}) %all-to-all-start.2) | async-done | bytes 2097184 | tf_op jit(solution)/shard_map/all_to_all | solution.py:324
  205.3 10.6 %all-to-all-start.3 = ((bf16[64,136,128]{2,1,0:T(8,128)(2,1)}), bf16[64,136,128]{2,1,0:T(8,128)(2,1)S(1)}, u32[]{:S(2)}, u32[]{:S(2)}) async-start(bf16[64,136,128]{2,1,0:T(8,128)(2,1)} %copy-done), calls=%async_computation.3 | async-start | bytes 4456448 | tf_op jit(solution)/shard_map/all_to_all | solution.py:324
  215.9 0.0 copy-done.6
  215.9 16.2 %shard_map.85 = (f32[16,64,128]{2,1,0:T(8,128)S(1)}, f32[16,64,128]{2,1,0:T(8,128)S(1)}) custom-call(bf16[16,64,128]{2,1,0:T(8,128)(2,1)S(1)} %bitcast.16, bf16[16,2,8,128]{3,2,1,0:T(8,128)(2,1)S(1)} %bitcast.17, bf16[64,2,64,128]{3,2,1,0:T(8,128)(2,1)} %bitcast.6.hot_ref), custom_call_target="tpu_custom_call" | custom-call | flops 2147483648 | bytes 2097152 | tf_op jit(solution)/shard_map/pallas_call | solution.py:241
  232.2 37.5 %all-to-all-done.3.served_ref = bf16[64,136,128]{2,1,0:T(8,128)(2,1)S(1)} async-done(((bf16[64,136,128]{2,1,0:T(8,128)(2,1)}), bf16[64,136,128]{2,1,0:T(8,128)(2,1)S(1)}, u32[]{:S(2)}, u32[]{:S(2)}) %all-to-all-start.3) | async-done | bytes 2228256 | tf_op jit(solution)/shard_map/all_to_all | solution.py:324
  269.7 5.5 %shard_map.86 = bf16[16,64,128]{2,1,0:T(8,128)(2,1)} custom-call(s32[128]{0:T(128)S(1)} %get-tuple-element.15.slot_ref, bf16[64,136,128]{2,1,0:T(8,128)(2,1)S(1)} %all-to-all-done.3.served_ref, f32[16,64,128]{2,1,0:T(8,128)S(1)} %get-tuple-element.23.mix_ref, f32[16,64,128]{2,1,0:T(8,128)S(1)} %get-tuple-element.24.stat_ref), custom_call_target="tpu_custom_call" | custom-call | tf_op jit(solution)/shard_map/pallas_call | solution.py:313
  (2 shorter events, 0.0 us)
Async XLA Ops:
  0.0 0.7 copy-start.3
  4.5 16.8 %copy-start.7 = (s32[16,8]{0,1:T(8,128)S(1)}, s32[16,8]{0,1:T(8,128)}, u32[]{:S(2)}) copy-start(s32[16,8]{0,1:T(8,128)} %param.12) | copy-start | bytes 1540
  4.5 16.8 %copy-start.8 = (s32[16,8]{0,1:T(8,128)S(1)}, s32[16,8]{0,1:T(8,128)}, u32[]{:S(2)}) copy-start(s32[16,8]{0,1:T(8,128)} %param.13) | copy-start | bytes 1540
  4.5 16.9 %copy-start.2 = (bf16[16,8,8,128]{3,2,1,0:T(8,128)(2,1)S(1)}, bf16[16,8,8,128]{3,2,1,0:T(8,128)(2,1)}, u32[]{:S(2)}) copy-start(bf16[16,8,8,128]{3,2,1,0:T(8,128)(2,1)} %param.8) | copy-start | bytes 786436
  4.5 16.9 %copy-start.4 = (s32[16]{0:T(128)S(1)}, s32[16]{0:T(128)}, u32[]{:S(2)}) copy-start(s32[16]{0:T(128)} %len_ref.1) | copy-start | bytes 196
  4.5 68.7 %all-to-all-start = ((bf16[64,128,128]{2,1,0:T(8,128)(2,1)}), bf16[64,128,128]{2,1,0:T(8,128)(2,1)S(1)}, u32[]{:S(2)}, u32[]{:S(2)}) async-start(bf16[64,128,128]{2,1,0:T(8,128)(2,1)} %shard_map.83), calls=%async_computation | async-start | bytes 4194304 | tf_op jit(solution)/shard_map/all_to_all | solution.py:324
  27.2 1.4 copy-start.1
  73.2 1.3 copy-start.5
  74.5 64.6 %all-to-all-start.1 = ((bf16[64,136,128]{2,1,0:T(8,128)(2,1)}), bf16[64,136,128]{2,1,0:T(8,128)(2,1)S(1)}, u32[]{:S(2)}, u32[]{:S(2)}) async-start(bf16[64,136,128]{2,1,0:T(8,128)(2,1)} %copy-done.1), calls=%async_computation.1 | async-start | bytes 4456448 | tf_op jit(solution)/shard_map/all_to_all | solution.py:324
  140.9 64.3 %all-to-all-start.2 = ((bf16[64,128,128]{2,1,0:T(8,128)(2,1)}), bf16[64,128,128]{2,1,0:T(8,128)(2,1)}, u32[]{:S(2)}, u32[]{:S(2)}) async-start(bf16[64,128,128]{2,1,0:T(8,128)(2,1)} %broadcast_in_dim.3), calls=%async_computation.2 | async-start | bytes 4194304 | tf_op jit(solution)/shard_map/all_to_all | solution.py:324
  167.2 1.4 copy-start
  168.6 47.3 %copy-start.6 = (bf16[16,8,1,2,128]{4,3,2,1,0:T(2,128)(2,1)S(1)}, bf16[16,8,1,2,128]{4,3,2,1,0:T(2,128)(2,1)}, u32[]{:S(2)}) copy-start(bf16[16,8,1,2,128]{4,3,2,1,0:T(2,128)(2,1)} %param.9) | copy-start | bytes 196612
  205.3 64.4 %all-to-all-start.3 = ((bf16[64,136,128]{2,1,0:T(8,128)(2,1)}), bf16[64,136,128]{2,1,0:T(8,128)(2,1)S(1)}, u32[]{:S(2)}, u32[]{:S(2)}) async-start(bf16[64,136,128]{2,1,0:T(8,128)(2,1)} %copy-done), calls=%async_computation.3 | async-start | bytes 4456448 | tf_op jit(solution)/shard_map/all_to_all | solution.py:324

commit v4 on v1

v4 whole, which is shorter than its diff:
```python
import functools
import math

import jax
import jax.numpy as jnp
from jax import lax
from jax.experimental import pallas as pl
from jax.experimental.pallas import tpu as pltpu
from jax.sharding import PartitionSpec as P

NEG_FILL = -1e30
CAP = 2
EXTRA = 8
NEAR_WEIGHT = 64
MERGE_BLOCK = 2
VMEM_LIMIT = 48 * 1024 * 1024

SMEM_SPEC = pl.BlockSpec(memory_space=pltpu.SMEM)
VMEM_SPEC = pl.BlockSpec(memory_space=pltpu.VMEM)


def deal_kernel(hot_ref, pool_ref, out_ref):
    def one(i, carry):
        page = jnp.clip(hot_ref[i], 0, pool_ref.shape[0] - 1)
        for part in range(2):
            out_ref[2 * i + part] = pool_ref[page, part]
        return carry

    lax.fori_loop(0, hot_ref.shape[0], one, 0)


def deal(hot_pages, pool):
    _, two, page_len, head_dim = pool.shape
    return pl.pallas_call(
        deal_kernel,
        out_shape=jax.ShapeDtypeStruct((two * hot_pages.shape[0], page_len, head_dim), pool.dtype),
        in_specs=[SMEM_SPEC, VMEM_SPEC],
        out_specs=VMEM_SPEC,
        compiler_params=pltpu.CompilerParams(vmem_limit_bytes=VMEM_LIMIT),
    )(hot_pages, pool)


def ask_kernel(len_ref, holder_ref, index_ref, q_ref, ask_ref, slot_ref, count_ref, *, page_len):
    requests, max_pages = holder_ref.shape
    groups = ask_ref.shape[0]
    rows = q_ref.shape[1]
    body = CAP * rows
    lanes = ask_ref.shape[2]

    def clear(g, carry):
        count_ref[g] = 0
        ask_ref[g, pl.ds(body, EXTRA), :] = jnp.zeros((EXTRA, lanes), ask_ref.dtype)
        return carry

    lax.fori_loop(0, groups, clear, 0)
    sub = lax.broadcasted_iota(jnp.int32, (EXTRA, lanes), 0)
    lane = lax.broadcasted_iota(jnp.int32, (EXTRA, lanes), 1)

    def one(i, carry):
        r = i // max_pages
        p = i - r * max_pages
        filled = jnp.clip(len_ref[r] - p * page_len, 0, page_len)
        slot_ref[i] = -1

        @pl.when(filled > 0)
        def _():
            h = holder_ref[r, p]
            rank = jnp.minimum(count_ref[h], CAP - 1)
            count_ref[h] = rank + 1
            slot_ref[i] = h * CAP + rank
            ask_ref[h, pl.ds(pl.multiple_of(rank * rows, rows), rows), :] = q_ref[r]
            page = index_ref[r, p].astype(jnp.float32)
            old = ask_ref[h, pl.ds(body, EXTRA), :].astype(jnp.float32)
            new = jnp.where(lane == 0, page, filled.astype(jnp.float32))
            ask_ref[h, pl.ds(body, EXTRA), :] = jnp.where(
                (sub == rank) & (lane < 2), new, old
            ).astype(ask_ref.dtype)

        return carry

    lax.fori_loop(0, requests * max_pages, one, 0)


def ask(context_len, page_holder, page_index, q, groups, page_len):
    requests, max_pages = page_holder.shape
    rows, lanes = q.shape[1:]
    return pl.pallas_call(
        functools.partial(ask_kernel, page_len=page_len),
        out_shape=(
            jax.ShapeDtypeStruct((groups, CAP * rows + EXTRA, lanes), q.dtype),
            jax.ShapeDtypeStruct((requests * max_pages,), jnp.int32),
        ),
        in_specs=[SMEM_SPEC, SMEM_SPEC, SMEM_SPEC, VMEM_SPEC],
        out_specs=(VMEM_SPEC, SMEM_SPEC),
        scratch_shapes=[pltpu.SMEM((groups,), jnp.int32)],
        compiler_params=pltpu.CompilerParams(vmem_limit_bytes=VMEM_LIMIT),
    )(context_len, page_holder, page_index, q)


def serve_kernel(table_ref, asked_ref, pool_ref, out_ref, *, factor, block):
    groups, tall, lanes = asked_ref.shape
    body = tall - EXTRA
    rows = body // CAP
    page_len = pool_ref.shape[2]
    token = lax.broadcasted_iota(jnp.int32, (rows, page_len), 1)
    column = lax.broadcasted_iota(jnp.int32, (body, lanes), 1)
    sub = lax.broadcasted_iota(jnp.int32, (EXTRA, lanes), 0)

    def one(step, carry):
        scores = []
        pages = []
        for g in range(block):
            for s in range(CAP):
                at = ((step * block + g) * CAP + s) * 2
                page = jnp.clip(table_ref[at], 0, pool_ref.shape[0] - 1)
                sc = lax.dot_general(
                    asked_ref[step * block + g, s * rows : (s + 1) * rows, :],
                    pool_ref[page, 0],
                    (((1,), (1,)), ((), ())),
                    preferred_element_type=jnp.float32,
                )
                scores.append(jnp.where(token < table_ref[at + 1], sc * factor, NEG_FILL))
                pages.append(page)
        stats = jnp.zeros((body, lanes), jnp.float32)
        for g in range(block):
            both = []
            for s in range(CAP):
                sc = scores[g * CAP + s]
                top = jnp.max(sc, axis=1, keepdims=True)
                ex = jnp.exp2(sc - top)
                total = jnp.sum(ex, axis=1, keepdims=True)
                mix = jnp.dot(
                    ex.astype(jnp.bfloat16),
                    pool_ref[pages[g * CAP + s], 1],
                    preferred_element_type=jnp.float32,
                )
                out_ref[step * block + g, s * rows : (s + 1) * rows, :] = (
                    mix * (1.0 / total)
                ).astype(out_ref.dtype)
                both.append(top + jnp.log2(total))
            stats = jnp.where(column == g, jnp.concatenate(both, axis=0), stats)
        flat = stats.T
        high = flat.astype(jnp.bfloat16).astype(jnp.float32)
        low = flat - high
        for g in range(block):
            tile = jnp.where(sub == 0, high[g : g + 1], jnp.where(sub == 1, low[g : g + 1], 0.0))
            out_ref[step * block + g, body : body + EXTRA, :] = tile.astype(out_ref.dtype)
        return carry

    lax.fori_loop(0, groups // block, one, 0)


def serve(table, asked, pool, factor):
    block = math.gcd(asked.shape[0], 16)
    return pl.pallas_call(
        functools.partial(serve_kernel, factor=factor, block=block),
        out_shape=jax.ShapeDtypeStruct(asked.shape, asked.dtype),
        in_specs=[SMEM_SPEC, VMEM_SPEC, VMEM_SPEC],
        out_specs=VMEM_SPEC,
        compiler_params=pltpu.CompilerParams(vmem_limit_bytes=VMEM_LIMIT),
    )(table, asked, pool)


def near_kernel(q_ref, fresh_ref, hot_ref, mix_ref, stat_ref, kv_ref, *, factor, per_kv, block):
    page_len = hot_ref.shape[1]
    chunks, _, chunk, _ = kv_ref.shape
    per_chunk = chunk // page_len

    def lay(c, carry):
        for i in range(per_chunk):
            for part in range(2):
                kv_ref[c, part, i * page_len : (i + 1) * page_len, :] = hot_ref[
                    2 * (c * per_chunk + i) + part
                ]
        return carry

    lax.fori_loop(0, chunks, lay, 0)
    requests, rows, lanes = q_ref.shape
    steps = fresh_ref.shape[2]
    rhs_t = (((1,), (1,)), ((), ()))
    row_step = lax.broadcasted_iota(jnp.int32, (rows, steps), 0) // per_kv
    key_step = lax.broadcasted_iota(jnp.int32, (rows, steps), 1)

    def one(n, carry):
        at = pl.ds(n * block, block)
        own = q_ref[at]
        q = own.reshape(block * rows, lanes)
        fresh_scores = []
        for b in range(block):
            sc = lax.dot_general(
                own[b], fresh_ref[n * block + b, 0], rhs_t, preferred_element_type=jnp.float32
            )
            fresh_scores.append(jnp.where(key_step <= row_step, sc * factor, NEG_FILL))
        sc = jnp.concatenate(fresh_scores, axis=0)
        top = jnp.max(sc, axis=1, keepdims=True)
        ex = jnp.exp2(sc - top)
        total = jnp.sum(ex, axis=1, keepdims=True)
        weights = ex.astype(jnp.bfloat16)
        mix = jnp.concatenate(
            [
                jnp.dot(
                    weights[b * rows : (b + 1) * rows],
                    fresh_ref[n * block + b, 1],
                    preferred_element_type=jnp.float32,
                )
                for b in range(block)
            ],
            axis=0,
        )
        for c in range(chunks):
            sc = lax.dot_general(q, kv_ref[c, 0], rhs_t, preferred_element_type=jnp.float32)
            new_top = jnp.maximum(top, jnp.max(sc, axis=1, keepdims=True) * factor)
            ex = jnp.exp2(sc * factor - new_top)
            keep = jnp.exp2(top - new_top)
            total = total * keep + jnp.sum(ex, axis=1, keepdims=True)
            mix = mix * keep + jnp.dot(
                ex.astype(jnp.bfloat16), kv_ref[c, 1], preferred_element_type=jnp.float32
            )
            top = new_top
        mix_ref[at] = (mix / total).reshape(block, rows, lanes)
        lse = top + jnp.log2(total)
        stat_ref[at] = jnp.broadcast_to(lse, (block * rows, lanes)).reshape(block, rows, lanes)
        return carry

    lax.fori_loop(0, requests // block, one, 0)


def near(q, fresh, hot, factor, per_kv):
    requests, rows, lanes = q.shape
    tokens = hot.shape[0] // 2 * hot.shape[1]
    block = math.gcd(requests, 8)
    chunks = math.gcd(hot.shape[0] // 2, 8)
    return pl.pallas_call(
        functools.partial(near_kernel, factor=factor, per_kv=per_kv, block=block),
        out_shape=(
            jax.ShapeDtypeStruct(q.shape, jnp.float32),
            jax.ShapeDtypeStruct(q.shape, jnp.float32),
        ),
        in_specs=[VMEM_SPEC] * 3,
        out_specs=(VMEM_SPEC, VMEM_SPEC),
        scratch_shapes=[pltpu.VMEM((chunks, 2, tokens // chunks, lanes), hot.dtype)],
        compiler_params=pltpu.CompilerParams(vmem_limit_bytes=VMEM_LIMIT),
        cost_estimate=pl.CostEstimate(
            flops=NEAR_WEIGHT * 4 * requests * rows * tokens * lanes,
            bytes_accessed=2 * tokens * lanes * 2,
            transcendentals=requests * rows * tokens,
        ),
    )(q, fresh, hot)


def merge_kernel(slot_ref, served_ref, mix_ref, stat_ref, out_ref, lse_ref, *, max_pages):
    groups = served_ref.shape[0]
    requests, rows, lanes = mix_ref.shape
    block = math.gcd(requests, MERGE_BLOCK)
    body = CAP * rows

    def unpack(g, carry):
        tile = served_ref[g, pl.ds(body, EXTRA), :].astype(jnp.float32)
        lse_ref[pl.ds(g, 1), :] = tile[0:1] + tile[1:2]
        return carry

    lax.fori_loop(0, groups, unpack, 0)
    lse_ref[pl.ds(body, body), :] = lse_ref[pl.ds(0, body), :].T
    column = lax.broadcasted_iota(jnp.int32, (rows, lanes), 1)

    def one(n, carry):
        for b in range(block):
            merge_one(n * block + b)
        return carry

    def merge_one(r):
        own = stat_ref[r]
        own_top = jnp.max(own, axis=1, keepdims=True)
        tops = []
        for p in range(max_pages):
            slot = slot_ref[r * max_pages + p]
            safe = jnp.maximum(slot, 0)
            h = safe // CAP
            rank = safe - h * CAP
            picked = lse_ref[pl.ds(pl.multiple_of(body + rank * rows, rows), rows), :]
            lse = jnp.sum(jnp.where(column == h, picked, 0.0), axis=1, keepdims=True)
            tops.append(jnp.where(slot >= 0, lse, NEG_FILL))
        top = own_top
        for p in range(max_pages):
            top = jnp.maximum(top, tops[p])
        weight = jnp.exp2(own_top - top)
        total = weight
        mix = mix_ref[r] * weight
        for p in range(max_pages):
            slot = slot_ref[r * max_pages + p]
            safe = jnp.maximum(slot, 0)
            h = safe // CAP
            rank = safe - h * CAP
            weight = jnp.exp2(tops[p] - top)
            total = total + weight
            part = served_ref[h, pl.ds(pl.multiple_of(rank * rows, rows), rows), :]
            mix = mix + jnp.where(slot >= 0, part.astype(jnp.float32) * weight, 0.0)
        out_ref[r] = (mix / total).astype(out_ref.dtype)

    lax.fori_loop(0, requests // block, one, 0)


def merge(slots, served, mix, stat, max_pages):
    requests, rows, lanes = mix.shape
    return pl.pallas_call(
        functools.partial(merge_kernel, max_pages=max_pages),
        out_shape=jax.ShapeDtypeStruct(mix.shape, jnp.bfloat16),
        in_specs=[SMEM_SPEC, VMEM_SPEC, VMEM_SPEC, VMEM_SPEC],
        out_specs=VMEM_SPEC,
        scratch_shapes=[pltpu.VMEM((2 * CAP * rows, lanes), jnp.float32)],
        compiler_params=pltpu.CompilerParams(vmem_limit_bytes=VMEM_LIMIT),
    )(slots, served, mix, stat)


def exchange(value):
    return lax.all_to_all(value, "group", split_axis=0, concat_axis=0, tiled=True)


def on_device(
    queries, fresh_kv, page_pool, context_len, page_holder, page_index, hot_owner, hot_pages
):
    requests, steps, local_heads, head_dim = queries.shape
    max_pages = page_holder.shape[1]
    groups = lax.axis_size("group")
    factor = math.log2(math.e) / math.sqrt(head_dim)
    q = queries.reshape(requests, steps * local_heads, head_dim)
    fresh = fresh_kv[:, :, 0].transpose(0, 2, 1, 3)
    pool = page_pool[:, 0]
    body = CAP * steps * local_heads
    dealt = exchange(deal(hot_pages, pool))
    asked, slots = ask(context_len, page_holder, page_index, q, groups, page_pool.shape[3])
    asked, dealt = lax.optimization_barrier((asked, dealt))
    share = lax.dynamic_index_in_dim(dealt, hot_owner[0], 0, keepdims=False)
    hot = lax.all_gather(share, "group", axis=0, tiled=False)

    def attend(sent, pages):
        sent = exchange(sent)
        table = sent[:, body : body + CAP, 0:2].astype(jnp.int32).reshape(-1)
        return serve(table, sent, pages, factor)

    def nothing(sent, pages):
        return jnp.zeros_like(sent)

    served = lax.cond(hot_owner[0] >= 0, attend, nothing, asked, pool)
    served = exchange(served)
    mix, stat = near(q, fresh, hot, factor, local_heads)
    attended = merge(slots, served, mix, stat, max_pages)
    return attended.reshape(requests, steps, local_heads, head_dim)


def solution(mesh):
    placed = (
        P("group", None, "head", None),
        P("group", None, "head", None, None),
        P("group", "head", None, None, None),
        P("group"),
        P("group", None),
        P("group", None),
        P(),
        P(),
    )
    return jax.shard_map(
        on_device,
        mesh=mesh,
        in_specs=placed,
        out_specs=P("group", None, "head", None),
        check_vma=False,
    )
```

time: 338 us -> 266 us (0.79)
  waiting for transfers between devices: 187 us -> 120 us
  starting transfers between devices: 8.04 us -> 27.2 us
  local copies, waits for them, and re-layouts: 14.3 us -> 4.65 us
  blocking collectives: 75.5 us -> 67.1 us
  Pallas kernels: 38.1 us -> 32.6 us
    psum x1 -> x0, waiting for transfers between devices: 187 us -> none  [spread(): return lax.psum(kept, axis)]
    all_gather x0 -> x1, waiting for transfers between devices: none -> 75.2 us  [on_device(): hot = lax.all_gather(share, 'group', axis=0, tiled=False)]
    all_to_all x1 -> x2, waiting for transfers between devices: 0.01 us -> 44.5 us  [exchange(): lax.all_to_all(value, 'group', split_axis=0, concat_axis=0, tiled=True)]
    all_to_all x1 -> x2, starting transfers between devices: 8 us -> 27.2 us  [exchange(): lax.all_to_all(value, 'group', split_axis=0, concat_axis=0, tiled=True)]
    all_to_all x1, blocking collectives: 75.5 us -> 67.1 us  [exchange(): lax.all_to_all(value, 'group', split_axis=0, concat_axis=0, tiled=True)]
    pallas_call x2 -> x3, Pallas kernels: 26.8 us -> 21.8 us  [the longest x1 10.2 us: serve(): pl.pallas_call(functools.partial(serve_kernel, factor=factor, block=block...]
    unnamed x19, local copies, waits for them, and re-layouts: 8.38 us -> 3.89 us
    gather x1 -> x0, local copies, waits for them, and re-layouts: 4.32 us -> none  [on_device(): hot_local = jnp.take(pool, hot_pages, axis=0, mode='clip')]
  transfers between devices with their start and end apart: 2 -> 3, of which waited for: 1 -> 2; matrix products, arithmetic and copies ran while one was open for 2% -> 0% of each run, Pallas kernels for 4% -> 9%
where the time goes in v4:
time: 266 us
  waiting for transfers between devices  120 us (45%)
  blocking collectives  67.1 us (25%)
  Pallas kernels  32.6 us (12%)
  starting transfers between devices  27.2 us (10%)
  between operations  14.1 us (5%)
  local copies, waits for them, and re-layouts  4.65 us (2%)
    all_gather x1, waiting for transfers between devices, on_device(): hot = lax.all_gather(share, 'group', axis=0, tiled=False)  75.2 us
    all_to_all x1, blocking collectives, exchange(): lax.all_to_all(value, 'group', split_axis=0, concat_axis=0, tiled=True)  67.1 us
    all_to_all x2, waiting for transfers between devices, exchange(): lax.all_to_all(value, 'group', split_axis=0, concat_axis=0, tiled=True)  44.5 us
    all_to_all x2, starting transfers between devices, exchange(): lax.all_to_all(value, 'group', split_axis=0, concat_axis=0, tiled=True)  27.2 us
    pallas_call x1, Pallas kernels, serve(): pl.pallas_call(functools.partial(serve_kernel, factor=factor, block=block...  10.2 us
    pallas_call x1, Pallas kernels, near(): pl.pallas_call(functools.partial(near_kernel, factor=factor, per_kv=per_k...  7.69 us
    pallas_call x1, Pallas kernels, ask(): pl.pallas_call(functools.partial(ask_kernel, page_len=page_len), out_shap...  6.51 us
  transfers between devices with their start and end apart: 3, of which 2 were waited for; matrix products, arithmetic and copies ran while one was open for 0% of the time, Pallas kernels for 9%

profile of v4, /device:TPU:6, one launch (start us, length us, event | category | flops | bytes accessed | tf_op | source)
XLA Modules:
  0.0 265.5 jit_solution(10939746373287635150)
XLA Ops:
  6.5 0.0 copy-start.2
  6.5 0.7 copy-done.2
  7.2 3.8 %shard_map.83 = bf16[64,128,128]{2,1,0:T(8,128)(2,1)} custom-call(s32[32]{0:T(128)S(1)} %copy-done.2, bf16[64,2,128,128]{3,2,1,0:T(8,128)(2,1)} %bitcast.16), custom_call_target="tpu_custom_call" | custom-call | tf_op jit(solution)/shard_map/pallas_call | solution.py:34
  11.0 0.0 copy-start.6
  11.0 0.0 copy-start.7
  11.0 0.0 copy-start
  11.0 0.0 copy-start.3
  11.1 0.0 copy-start.5
  11.1 16.7 %all-to-all-start.1 = ((bf16[64,128,128]{2,1,0:T(8,128)(2,1)}), bf16[64,128,128]{2,1,0:T(8,128)(2,1)S(1)}, u32[]{:S(2)}, u32[]{:S(2)}) async-start(bf16[64,128,128]{2,1,0:T(8,128)(2,1)} %shard_map.83), calls=%async_computation.1 | async-start | bytes 4194304 | tf_op jit(solution)/shard_map/all_to_all | solution.py:316
  27.8 0.0 all-gather.2.cloned.1.call-start
  28.5 0.0 copy-done.6
  28.5 0.1 copy.15.holder_ref
  28.6 0.0 copy-done.7
  28.6 0.1 copy.16.index_ref
  28.7 0.0 copy-done
  28.7 0.0 copy-done.3
  28.7 6.5 %shard_map.82 = (bf16[64,136,128]{2,1,0:T(8,128)(2,1)}, s32[128]{0:T(128)S(1)}) custom-call(s32[16]{0:T(128)S(1)} %copy-done.3, s32[16,8]{1,0:T(8,128)S(1)} %copy.15.holder_ref, s32[16,8]{1,0:T(8,128)S(1)} %copy.16.index_ref, bf16[16,64,128]{2,1,0:T(8,128)(2,1)S(1)} %bitcast.13), custom_call_target="tpu_custom_call" | custom-call | tf_op jit(solution)/shard_map/pallas_call | solution.py:87
  35.2 44.5 %all-to-all-done.1 = bf16[64,128,128]{2,1,0:T(8,128)(2,1)S(1)} async-done(((bf16[64,128,128]{2,1,0:T(8,128)(2,1)}), bf16[64,128,128]{2,1,0:T(8,128)(2,1)S(1)}, u32[]{:S(2)}, u32[]{:S(2)}) %all-to-all-start.1) | async-done | bytes 2097184 | tf_op jit(solution)/shard_map/all_to_all | solution.py:316
  79.7 0.6 constant_dynamic-slice_fusion
  80.3 0.0 all-gather.2.cloned.1.call-update
  80.4 0.0 copy-done.5
  80.4 0.6 copy.19
  81.0 77.5 %conditional.1 = (bf16[64,136,128]{2,1,0:T(8,128)(2,1)}) conditional(s32[]{:T(128)} %convert_element_type.4, () %tuple.12, (bf16[64,136,128]{2,1,0:T(8,128)(2,1)}, bf16[64,2,128,128]{3,2,1,0:T(8,128)(2,1)}) %tuple.19), branch_computations={%region_0.1_spmd, %region_1.2_spmd} | conditional | flops 256 | bytes 4460040 | solution.py:344
  81.0 67.1 %all_to_all.14.asked_ref = bf16[64,136,128]{2,1,0:T(8,128)(2,1)S(1)} all-to-all(bf16[64,136,128]{2,1,0:T(8,128)(2,1)} %get-tuple-element.12), channel_id=1, replica_groups=mesh['group'=64,'head'=8] {'group'}, dimensions={0} | all-to-all | bytes 4456448 | tf_op jit(solution)/shard_map/cond/branch_1_fun/all_to_all | solution.py:316
  148.2 0.1 reshape.14.table_ref
  148.3 10.2 %branch_1_fun.1 = bf16[64,136,128]{2,1,0:T(8,128)(2,1)} custom-call(s32[256]{0:T(256)S(1)} %reshape.14.table_ref, bf16[64,136,128]{2,1,0:T(8,128)(2,1)S(1)} %all_to_all.14.asked_ref, bf16[64,2,128,128]{3,2,1,0:T(8,128)(2,1)} %get-tuple-element.13.pool_ref), custom_call_target="tpu_custom_call" | custom-call | tf_op jit(solution)/shard_map/cond/branch_1_fun/pallas_call | solution.py:155
  158.6 10.4 %all-to-all-start.2 = ((bf16[64,136,128]{2,1,0:T(8,128)(2,1)}), bf16[64,136,128]{2,1,0:T(8,128)(2,1)S(1)}, u32[]{:S(2)}, u32[]{:S(2)}) async-start(bf16[64,136,128]{2,1,0:T(8,128)(2,1)} %get-tuple-element.26), calls=%async_computation.2 | async-start | bytes 4456448 | tf_op jit(solution)/shard_map/all_to_all | solution.py:316
  169.0 75.2 %all-gather.2.cloned.1.call-done.hot_ref = bf16[64,128,128]{2,1,0:T(8,128)(2,1)} async-done(((bf16[1,128,128]{2,1,0:T(8,128)(2,1)}), bf16[64,128,128]{2,1,0:T(8,128)(2,1)}) %all-gather.2.cloned.1.call-update) | async-done | bytes 2097168 | tf_op jit(solution)/shard_map/all_gather | solution.py:334
  244.2 0.0 copy-start.1
  244.2 0.8 copy-done.1
  245.1 0.0 copy-start.4
  245.1 1.6 copy-done.4
  246.7 7.7 %shard_map.84 = (f32[16,64,128]{2,1,0:T(8,128)S(1)}, f32[16,64,128]{2,1,0:T(8,128)S(1)}) custom-call(bf16[16,64,128]{2,1,0:T(8,128)(2,1)S(1)} %bitcast.14, bf16[16,2,8,128]{3,2,1,0:T(8,128)(2,1)S(1)} %bitcast.15, bf16[64,128,128]{2,1,0:T(8,128)(2,1)S(1)} %copy-done.4), custom_call_target="tpu_custom_call" | custom-call | flops 137438953472 | bytes 2097152 | tf_op jit(solution)/shard_map/pallas_call | solution.py:233
  254.4 0.0 all-to-all-done.2.served_ref
  254.4 4.3 %shard_map.85 = bf16[16,64,128]{2,1,0:T(8,128)(2,1)} custom-call(s32[128]{0:T(128)S(1)} %get-tuple-element.20.slot_ref, bf16[64,136,128]{2,1,0:T(8,128)(2,1)S(1)} %all-to-all-done.2.served_ref, f32[16,64,128]{2,1,0:T(8,128)S(1)} %get-tuple-element.24.mix_ref, f32[16,64,128]{2,1,0:T(8,128)S(1)} %get-tuple-element.25.stat_ref), custom_call_target="tpu_custom_call" | custom-call | tf_op jit(solution)/shard_map/pallas_call | solution.py:305
  (1 shorter events, 0.0 us)
Async XLA Ops:
  6.5 0.7 copy-start.2
  11.0 17.5 %copy-start.6 = (s32[16,8]{0,1:T(8,128)S(1)}, s32[16,8]{0,1:T(8,128)}, u32[]{:S(2)}) copy-start(s32[16,8]{0,1:T(8,128)} %param.14) | copy-start | bytes 1540
  11.0 17.5 %copy-start.7 = (s32[16,8]{0,1:T(8,128)S(1)}, s32[16,8]{0,1:T(8,128)}, u32[]{:S(2)}) copy-start(s32[16,8]{0,1:T(8,128)} %param.15) | copy-start | bytes 1540
  11.0 17.6 %copy-start = (bf16[16,8,8,128]{3,2,1,0:T(8,128)(2,1)S(1)}, bf16[16,8,8,128]{3,2,1,0:T(8,128)(2,1)}, u32[]{:S(2)}) copy-start(bf16[16,8,8,128]{3,2,1,0:T(8,128)(2,1)} %param.10) | copy-start | bytes 786436
  11.0 17.6 %copy-start.3 = (s32[16]{0:T(128)S(1)}, s32[16]{0:T(128)}, u32[]{:S(2)}) copy-start(s32[16]{0:T(128)} %len_ref.1) | copy-start | bytes 196
  11.1 69.3 %copy-start.5 = (bf16[16,8,1,2,128]{4,3,2,1,0:T(2,128)(2,1)S(1)}, bf16[16,8,1,2,128]{4,3,2,1,0:T(2,128)(2,1)}, u32[]{:S(2)}) copy-start(bf16[16,8,1,2,128]{4,3,2,1,0:T(2,128)(2,1)} %param.11) | copy-start | bytes 196612
  11.1 68.7 %all-to-all-start.1 = ((bf16[64,128,128]{2,1,0:T(8,128)(2,1)}), bf16[64,128,128]{2,1,0:T(8,128)(2,1)S(1)}, u32[]{:S(2)}, u32[]{:S(2)}) async-start(bf16[64,128,128]{2,1,0:T(8,128)(2,1)} %shard_map.83), calls=%async_computation.1 | async-start | bytes 4194304 | tf_op jit(solution)/shard_map/all_to_all | solution.py:316
  27.8 216.4 %all-gather.2.cloned.1.call-start = ((), (), s32[]{:S(2)}) async-start(), calls=%async_computation.3 | async-start | bytes 2129920 | tf_op jit(solution)/shard_map/all_gather | solution.py:334
  158.6 95.8 %all-to-all-start.2 = ((bf16[64,136,128]{2,1,0:T(8,128)(2,1)}), bf16[64,136,128]{2,1,0:T(8,128)(2,1)S(1)}, u32[]{:S(2)}, u32[]{:S(2)}) async-start(bf16[64,136,128]{2,1,0:T(8,128)(2,1)} %get-tuple-element.26), calls=%async_computation.2 | async-start | bytes 4456448 | tf_op jit(solution)/shard_map/all_to_all | solution.py:316
  244.2 0.8 copy-start.1
  245.1 1.6 copy-start.4
Sparse Core Ops, SparseCore 0:
  80.5 163.6 all-gather.1

commit v5 on v4

--- a/solution.py
+++ b/solution.py
@@ -11,22 +11,26 @@
 NEG_FILL = -1e30
 CAP = 2
 EXTRA = 8
-NEAR_WEIGHT = 64
 MERGE_BLOCK = 2
 VMEM_LIMIT = 48 * 1024 * 1024
+HOT_VMEM_LIMIT = 56 * 1024 * 1024
 
 SMEM_SPEC = pl.BlockSpec(memory_space=pltpu.SMEM)
+HBM_SPEC = pl.BlockSpec(memory_space=pltpu.HBM)
 VMEM_SPEC = pl.BlockSpec(memory_space=pltpu.VMEM)
 
 
-def deal_kernel(hot_ref, pool_ref, out_ref):
-    def one(i, carry):
+def deal_kernel(hot_ref, pool_ref, out_ref, sems):
+    copies = []
+    for i in range(hot_ref.shape[0]):
         page = jnp.clip(hot_ref[i], 0, pool_ref.shape[0] - 1)
-        for part in range(2):
-            out_ref[2 * i + part] = pool_ref[page, part]
-        return carry
-
-    lax.fori_loop(0, hot_ref.shape[0], one, 0)
+        copies.append(
+            pltpu.make_async_copy(pool_ref.at[page], out_ref.at[pl.ds(2 * i, 2)], sems.at[i])
+        )
+    for copy in copies:
+        copy.start()
+    for copy in copies:
+        copy.wait()
 
 
 def deal(hot_pages, pool):
@@ -34,8 +38,9 @@
     return pl.pallas_call(
         deal_kernel,
         out_shape=jax.ShapeDtypeStruct((two * hot_pages.shape[0], page_len, head_dim), pool.dtype),
-        in_specs=[SMEM_SPEC, VMEM_SPEC],
+        in_specs=[SMEM_SPEC, HBM_SPEC],
         out_specs=VMEM_SPEC,
+        scratch_shapes=[pltpu.SemaphoreType.DMA((hot_pages.shape[0],))],
         compiler_params=pltpu.CompilerParams(vmem_limit_bytes=VMEM_LIMIT),
     )(hot_pages, pool)
 
@@ -161,155 +166,149 @@
     )(table, asked, pool)
 
 
-def near_kernel(q_ref, fresh_ref, hot_ref, mix_ref, stat_ref, kv_ref, *, factor, per_kv, block):
-    page_len = hot_ref.shape[1]
-    chunks, _, chunk, _ = kv_ref.shape
-    per_chunk = chunk // page_len
-
-    def lay(c, carry):
-        for i in range(per_chunk):
-            for part in range(2):
-                kv_ref[c, part, i * page_len : (i + 1) * page_len, :] = hot_ref[
-                    2 * (c * per_chunk + i) + part
-                ]
-        return carry
-
-    lax.fori_loop(0, chunks, lay, 0)
-    requests, rows, lanes = q_ref.shape
+def merge_kernel(
+    slot_ref, q_ref, fresh_ref, served_ref, mix_ref, stat_ref, lse_ref, *, factor, per_kv, max_pages
+):
+    groups = served_ref.shape[0]
+    requests, rows, lanes = mix_ref.shape
     steps = fresh_ref.shape[2]
-    rhs_t = (((1,), (1,)), ((), ()))
+    block = math.gcd(requests, MERGE_BLOCK)
+    body = CAP * rows
+
+    def unpack(g, carry):
+        tile = served_ref[g, pl.ds(body, EXTRA), :].astype(jnp.float32)
+        lse_ref[pl.ds(g, 1), :] = tile[0:1] + tile[1:2]
+        return carry
+
+    lax.fori_loop(0, groups, unpack, 0)
+    lse_ref[pl.ds(body, body), :] = lse_ref[pl.ds(0, body), :].T
+    column = lax.broadcasted_iota(jnp.int32, (rows, lanes), 1)
     row_step = lax.broadcasted_iota(jnp.int32, (rows, steps), 0) // per_kv
     key_step = lax.broadcasted_iota(jnp.int32, (rows, steps), 1)
 
     def one(n, carry):
-        at = pl.ds(n * block, block)
-        own = q_ref[at]
-        q = own.reshape(block * rows, lanes)
-        fresh_scores = []
         for b in range(block):
+            merge_one(n * block + b)
+        return carry
+
+    def merge_one(r):
+        sc = lax.dot_general(
+            q_ref[r],
+            fresh_ref[r, 0],
+            (((1,), (1,)), ((), ())),
+            preferred_element_type=jnp.float32,
+        )
+        sc = jnp.where(key_step <= row_step, sc * factor, NEG_FILL)
+        own_top = jnp.max(sc, axis=1, keepdims=True)
+        ex = jnp.exp2(sc - own_top)
+        own_total = jnp.sum(ex, axis=1, keepdims=True)
+        own = jnp.dot(
+            ex.astype(jnp.bfloat16), fresh_ref[r, 1], preferred_element_type=jnp.float32
+        )
+        places = []
+        tops = []
+        top = own_top
+        for p in range(max_pages):
+            slot = slot_ref[r * max_pages + p]
+            safe = jnp.maximum(slot, 0)
+            h = safe // CAP
+            start = pl.multiple_of((safe - h * CAP) * rows, rows)
+            picked = lse_ref[pl.ds(body + start, rows), :]
+            lse = jnp.sum(jnp.where(column == h, picked, 0.0), axis=1, keepdims=True)
+            lse = jnp.where(slot >= 0, lse, NEG_FILL)
+            places.append((slot, h, start))
+            tops.append(lse)
+            top = jnp.maximum(top, lse)
+        weight = jnp.exp2(own_top - top)
+        total = own_total * weight
+        mix = own * weight
+        for (slot, h, start), lse in zip(places, tops):
+            weight = jnp.exp2(lse - top)
+            total = total + weight
+            part = served_ref[h, pl.ds(start, rows), :]
+            mix = mix + jnp.where(slot >= 0, part.astype(jnp.float32) * weight, 0.0)
+        mix_ref[r] = mix
+        stat_ref[r] = jnp.where(column == 0, top, total)
+
+    lax.fori_loop(0, requests // block, one, 0)
+
+
+def merge(slots, q, fresh, served, factor, per_kv, max_pages):
+    requests, rows, lanes = q.shape
+    return pl.pallas_call(
+        functools.partial(merge_kernel, factor=factor, per_kv=per_kv, max_pages=max_pages),
+        out_shape=(
+            jax.ShapeDtypeStruct(q.shape, jnp.float32),
+            jax.ShapeDtypeStruct(q.shape, jnp.float32),
+        ),
+        in_specs=[SMEM_SPEC] + [VMEM_SPEC] * 3,
+        out_specs=(VMEM_SPEC, VMEM_SPEC),
+        scratch_shapes=[pltpu.VMEM((2 * CAP * rows, lanes), jnp.float32)],
+        compiler_params=pltpu.CompilerParams(vmem_limit_bytes=VMEM_LIMIT),
+    )(slots, q, fresh, served)
+
+
+def hot_kernel(q_ref, mix_ref, stat_ref, hot_ref, out_ref, kv_ref, sems, *, factor, block):
+    chunks, per_chunk, _, page_len, lanes = hot_ref.shape
+    copies = [
+        [
+            pltpu.make_async_copy(hot_ref.at[c, :, part], kv_ref.at[c, part], sems.at[c, part])
+            for part in range(2)
+        ]
+        for c in range(chunks)
+    ]
+    for pair in copies:
+        for copy in pair:
+            copy.start()
+    requests, rows, _ = q_ref.shape
+    for n in range(requests // block):
+        at = slice(n * block, (n + 1) * block)
+        q = q_ref[at].reshape(block * rows, lanes)
+        stat = stat_ref[at].reshape(block * rows, lanes)
+        top = stat[:, 0:1]
+        total = stat[:, 1:2]
+        mix = mix_ref[at].reshape(block * rows, lanes)
+        for c in range(chunks):
+            if n == 0:
+                for copy in copies[c]:
+                    copy.wait()
             sc = lax.dot_general(
-                own[b], fresh_ref[n * block + b, 0], rhs_t, preferred_element_type=jnp.float32
+                q,
+                kv_ref[c, 0].reshape(per_chunk * page_len, lanes),
+                (((1,), (1,)), ((), ())),
+                preferred_element_type=jnp.float32,
             )
-            fresh_scores.append(jnp.where(key_step <= row_step, sc * factor, NEG_FILL))
-        sc = jnp.concatenate(fresh_scores, axis=0)
-        top = jnp.max(sc, axis=1, keepdims=True)
-        ex = jnp.exp2(sc - top)
-        total = jnp.sum(ex, axis=1, keepdims=True)
-        weights = ex.astype(jnp.bfloat16)
-        mix = jnp.concatenate(
-            [
-                jnp.dot(
-                    weights[b * rows : (b + 1) * rows],
-                    fresh_ref[n * block + b, 1],
-                    preferred_element_type=jnp.float32,
-                )
-                for b in range(block)
-            ],
-            axis=0,
-        )
-        for c in range(chunks):
-            sc = lax.dot_general(q, kv_ref[c, 0], rhs_t, preferred_element_type=jnp.float32)
             new_top = jnp.maximum(top, jnp.max(sc, axis=1, keepdims=True) * factor)
             ex = jnp.exp2(sc * factor - new_top)
             keep = jnp.exp2(top - new_top)
             total = total * keep + jnp.sum(ex, axis=1, keepdims=True)
             mix = mix * keep + jnp.dot(
-                ex.astype(jnp.bfloat16), kv_ref[c, 1], preferred_element_type=jnp.float32
+                ex.astype(jnp.bfloat16),
+                kv_ref[c, 1].reshape(per_chunk * page_len, lanes),
+                preferred_element_type=jnp.float32,
             )
             top = new_top
-        mix_ref[at] = (mix / total).reshape(block, rows, lanes)
-        lse = top + jnp.log2(total)
-        stat_ref[at] = jnp.broadcast_to(lse, (block * rows, lanes)).reshape(block, rows, lanes)
-        return carry
-
-    lax.fori_loop(0, requests // block, one, 0)
-
-
-def near(q, fresh, hot, factor, per_kv):
+        out_ref[at] = (mix / total).astype(out_ref.dtype).reshape(block, rows, lanes)
+
+
+def attend_hot(q, mix, stat, hot, factor):
     requests, rows, lanes = q.shape
-    tokens = hot.shape[0] // 2 * hot.shape[1]
+    pages = hot.shape[0] // 2
+    page_len = hot.shape[1]
     block = math.gcd(requests, 8)
-    chunks = math.gcd(hot.shape[0] // 2, 8)
-    return pl.pallas_call(
-        functools.partial(near_kernel, factor=factor, per_kv=per_kv, block=block),
-        out_shape=(
-            jax.ShapeDtypeStruct(q.shape, jnp.float32),
-            jax.ShapeDtypeStruct(q.shape, jnp.float32),
-        ),
-        in_specs=[VMEM_SPEC] * 3,
-        out_specs=(VMEM_SPEC, VMEM_SPEC),
-        scratch_shapes=[pltpu.VMEM((chunks, 2, tokens // chunks, lanes), hot.dtype)],
-        compiler_params=pltpu.CompilerParams(vmem_limit_bytes=VMEM_LIMIT),
-        cost_estimate=pl.CostEstimate(
-            flops=NEAR_WEIGHT * 4 * requests * rows * tokens * lanes,
-            bytes_accessed=2 * tokens * lanes * 2,
-            transcendentals=requests * rows * tokens,
-        ),
-    )(q, fresh, hot)
-
-
-def merge_kernel(slot_ref, served_ref, mix_ref, stat_ref, out_ref, lse_ref, *, max_pages):
-    groups = served_ref.shape[0]
-    requests, rows, lanes = mix_ref.shape
-    block = math.gcd(requests, MERGE_BLOCK)
-    body = CAP * rows
-
-    def unpack(g, carry):
-        tile = served_ref[g, pl.ds(body, EXTRA), :].astype(jnp.float32)
-        lse_ref[pl.ds(g, 1), :] = tile[0:1] + tile[1:2]
-        return carry
-
-    lax.fori_loop(0, groups, unpack, 0)
-    lse_ref[pl.ds(body, body), :] = lse_ref[pl.ds(0, body), :].T
-    column = lax.broadcasted_iota(jnp.int32, (rows, lanes), 1)
-
-    def one(n, carry):
-        for b in range(block):
-            merge_one(n * block + b)
-        return carry
-
-    def merge_one(r):
-        own = stat_ref[r]
-        own_top = jnp.max(own, axis=1, keepdims=True)
-        tops = []
-        for p in range(max_pages):
-            slot = slot_ref[r * max_pages + p]
-            safe = jnp.maximum(slot, 0)
-            h = safe // CAP
-            rank = safe - h * CAP
-            picked = lse_ref[pl.ds(pl.multiple_of(body + rank * rows, rows), rows), :]
-            lse = jnp.sum(jnp.where(column == h, picked, 0.0), axis=1, keepdims=True)
-            tops.append(jnp.where(slot >= 0, lse, NEG_FILL))
-        top = own_top
-        for p in range(max_pages):
-            top = jnp.maximum(top, tops[p])
-        weight = jnp.exp2(own_top - top)
-        total = weight
-        mix = mix_ref[r] * weight
-        for p in range(max_pages):
-            slot = slot_ref[r * max_pages + p]
-            safe = jnp.maximum(slot, 0)
-            h = safe // CAP
-            rank = safe - h * CAP
-            weight = jnp.exp2(tops[p] - top)
-            total = total + weight
-            part = served_ref[h, pl.ds(pl.multiple_of(rank * rows, rows), rows), :]
-            mix = mix + jnp.where(slot >= 0, part.astype(jnp.float32) * weight, 0.0)
-        out_ref[r] = (mix / total).astype(out_ref.dtype)
-
-    lax.fori_loop(0, requests // block, one, 0)
-
-
-def merge(slots, served, mix, stat, max_pages):
-    requests, rows, lanes = mix.shape
-    return pl.pallas_call(
-        functools.partial(merge_kernel, max_pages=max_pages),
-        out_shape=jax.ShapeDtypeStruct(mix.shape, jnp.bfloat16),
-        in_specs=[SMEM_SPEC, VMEM_SPEC, VMEM_SPEC, VMEM_SPEC],
+    chunks = math.gcd(pages, 8)
+    hot = hot.reshape(chunks, pages // chunks, 2, page_len, lanes)
+    return pl.pallas_call(
+        functools.partial(hot_kernel, factor=factor, block=block),
+        out_shape=jax.ShapeDtypeStruct(q.shape, q.dtype),
+        in_specs=[VMEM_SPEC] * 3 + [HBM_SPEC],
         out_specs=VMEM_SPEC,
-        scratch_shapes=[pltpu.VMEM((2 * CAP * rows, lanes), jnp.float32)],
-        compiler_params=pltpu.CompilerParams(vmem_limit_bytes=VMEM_LIMIT),
-    )(slots, served, mix, stat)
+        scratch_shapes=[
+            pltpu.VMEM((chunks, 2, pages // chunks, page_len, lanes), hot.dtype),
+            pltpu.SemaphoreType.DMA((chunks, 2)),
+        ],
+        compiler_params=pltpu.CompilerParams(vmem_limit_bytes=HOT_VMEM_LIMIT),
+    )(q, mix, stat, hot)
 
 
 def exchange(value):
@@ -343,8 +342,8 @@
 
     served = lax.cond(hot_owner[0] >= 0, attend, nothing, asked, pool)
     served = exchange(served)
-    mix, stat = near(q, fresh, hot, factor, local_heads)
-    attended = merge(slots, served, mix, stat, max_pages)
+    mix, stat = merge(slots, q, fresh, served, factor, local_heads, max_pages)
+    attended = attend_hot(q, mix, stat, hot, factor)
     return attended.reshape(requests, steps, local_heads, head_dim)
 
 

time: 266 us -> 316 us (1.19)
  waiting for transfers between devices: 120 us -> 151 us
  Pallas kernels: 32.6 us -> 51.1 us
    all_to_all x2, waiting for transfers between devices: 44.5 us -> 97.2 us  [exchange(): lax.all_to_all(value, 'group', split_axis=0, concat_axis=0, tiled=True)]
    all_gather x1, waiting for transfers between devices: 75.2 us -> 54.1 us  [on_device(): hot = lax.all_gather(share, 'group', axis=0, tiled=False)]
    pallas_call x2, Pallas kernels: 12 us -> 30.7 us  [the longest x1 24.5 us: attend_hot(): pl.pallas_call(functools.partial(hot_kernel, factor=factor, block=block),...]
  transfers between devices with their start and end apart: 3 -> 3, of which waited for: 2 -> 3; matrix products, arithmetic and copies ran while one was open for 0% -> 0% of each run, Pallas kernels for 9% -> 4%
where the time goes in v5:
time: 316 us; the launch traced here: 315 us
  waiting for transfers between devices  151 us (48%)
  blocking collectives  68 us (22%)
  Pallas kernels  51.1 us (16%)
  starting transfers between devices  25.3 us (8%)
  between operations  14.2 us (4%)
  local copies, waits for them, and re-layouts  5.32 us (2%)
    all_to_all x2, waiting for transfers between devices, exchange(): lax.all_to_all(value, 'group', split_axis=0, concat_axis=0, tiled=True)  97.2 us
    all_to_all x1, blocking collectives, exchange(): lax.all_to_all(value, 'group', split_axis=0, concat_axis=0, tiled=True)  68 us
    all_gather x1, waiting for transfers between devices, on_device(): hot = lax.all_gather(share, 'group', axis=0, tiled=False)  54.1 us
    all_to_all x2, starting transfers between devices, exchange(): lax.all_to_all(value, 'group', split_axis=0, concat_axis=0, tiled=True)  25.2 us
    pallas_call x1, Pallas kernels, attend_hot(): pl.pallas_call(functools.partial(hot_kernel, factor=factor, block=block),...  24.5 us
    pallas_call x1, Pallas kernels, serve(): pl.pallas_call(functools.partial(serve_kernel, factor=factor, block=block...  10.1 us
    pallas_call x1, Pallas kernels, ask(): pl.pallas_call(functools.partial(ask_kernel, page_len=page_len), out_shap...  6.58 us
  transfers between devices with their start and end apart: 3, of which 3 were waited for; matrix products, arithmetic and copies ran while one was open for 0% of the time, Pallas kernels for 4%

profile of v5, /device:TPU:6, one launch (start us, length us, event | category | flops | bytes accessed | tf_op | source)
XLA Modules:
  0.0 315.2 jit_solution(7922665753138115989)
XLA Ops:
  6.5 0.0 copy-start.3
  6.5 0.7 copy-done.3
  7.2 3.7 %shard_map.83 = bf16[64,128,128]{2,1,0:T(8,128)(2,1)} custom-call(s32[32]{0:T(128)S(1)} %copy-done.3, bf16[64,2,128,128]{3,2,1,0:T(8,128)(2,1)} %bitcast.18), custom_call_target="tpu_custom_call" | custom-call | tf_op jit(solution)/shard_map/pallas_call | solution.py:38
  10.9 0.0 copy-start.7
  10.9 0.0 copy-start.8
  10.9 0.0 copy-start
  10.9 0.0 copy-start.4
  10.9 16.7 %all-to-all-start.1 = ((bf16[64,128,128]{2,1,0:T(8,128)(2,1)}), bf16[64,128,128]{2,1,0:T(8,128)(2,1)S(1)}, u32[]{:S(2)}, u32[]{:S(2)}) async-start(bf16[64,128,128]{2,1,0:T(8,128)(2,1)} %shard_map.83), calls=%async_computation.1 | async-start | bytes 4194304 | tf_op jit(solution)/shard_map/all_to_all | solution.py:315
  27.7 0.0 copy-done.7
  27.7 0.1 copy.15.holder_ref
  27.8 0.0 copy-done.8
  27.8 0.1 copy.16.index_ref
  28.5 0.0 copy-done
  28.5 0.0 copy-done.4
  28.5 6.6 %shard_map.82 = (bf16[64,136,128]{2,1,0:T(8,128)(2,1)}, s32[128]{0:T(128)S(1)}) custom-call(s32[16]{0:T(128)S(1)} %copy-done.4, s32[16,8]{1,0:T(8,128)S(1)} %copy.15.holder_ref, s32[16,8]{1,0:T(8,128)S(1)} %copy.16.index_ref, bf16[16,64,128]{2,1,0:T(8,128)(2,1)S(1)} %bitcast.15), custom_call_target="tpu_custom_call" | custom-call | tf_op jit(solution)/shard_map/pallas_call | solution.py:92
  35.1 44.5 %all-to-all-done.1 = bf16[64,128,128]{2,1,0:T(8,128)(2,1)S(1)} async-done(((bf16[64,128,128]{2,1,0:T(8,128)(2,1)}), bf16[64,128,128]{2,1,0:T(8,128)(2,1)S(1)}, u32[]{:S(2)}, u32[]{:S(2)}) %all-to-all-start.1) | async-done | bytes 2097184 | tf_op jit(solution)/shard_map/all_to_all | solution.py:315
  79.6 0.0 copy-start.5
  79.6 1.4 copy-done.5
  81.0 78.3 %conditional.1 = (bf16[64,136,128]{2,1,0:T(8,128)(2,1)}) conditional(s32[]{:T(128)} %convert_element_type.4, () %tuple.12, (bf16[64,136,128]{2,1,0:T(8,128)(2,1)}, bf16[64,2,128,128]{3,2,1,0:T(8,128)(2,1)}) %tuple.19), branch_computations={%region_0.1_spmd, %region_1.2_spmd} | conditional | flops 256 | bytes 4460040 | solution.py:343
  81.0 68.0 %all_to_all.14.asked_ref = bf16[64,136,128]{2,1,0:T(8,128)(2,1)S(1)} all-to-all(bf16[64,136,128]{2,1,0:T(8,128)(2,1)} %get-tuple-element.12), channel_id=1, replica_groups=mesh['group'=64,'head'=8] {'group'}, dimensions={0} | all-to-all | bytes 4456448 | tf_op jit(solution)/shard_map/cond/branch_1_fun/all_to_all | solution.py:315
  149.0 0.1 reshape.18.table_ref
  149.2 10.1 %branch_1_fun.1 = bf16[64,136,128]{2,1,0:T(8,128)(2,1)} custom-call(s32[256]{0:T(256)S(1)} %reshape.18.table_ref, bf16[64,136,128]{2,1,0:T(8,128)(2,1)S(1)} %all_to_all.14.asked_ref, bf16[64,2,128,128]{3,2,1,0:T(8,128)(2,1)} %get-tuple-element.13.pool_ref), custom_call_target="tpu_custom_call" | custom-call | tf_op jit(solution)/shard_map/cond/branch_1_fun/pallas_call | solution.py:160
  159.3 0.0 copy-start.6
  159.3 8.5 %all-to-all-start.2 = ((bf16[64,136,128]{2,1,0:T(8,128)(2,1)}), bf16[64,136,128]{2,1,0:T(8,128)(2,1)S(1)}, u32[]{:S(2)}, u32[]{:S(2)}) async-start(bf16[64,136,128]{2,1,0:T(8,128)(2,1)} %get-tuple-element.26), calls=%async_computation.2 | async-start | bytes 4456448 | tf_op jit(solution)/shard_map/all_to_all | solution.py:315
  167.8 0.0 all-gather.2.cloned.1.call-start
  167.9 1.4 constant_dynamic-slice_fusion
  169.2 0.0 all-gather.2.cloned.1.call-update
  169.3 0.0 copy-done.6
  169.3 52.7 %all-to-all-done.2.served_ref = bf16[64,136,128]{2,1,0:T(8,128)(2,1)S(1)} async-done(((bf16[64,136,128]{2,1,0:T(8,128)(2,1)}), bf16[64,136,128]{2,1,0:T(8,128)(2,1)S(1)}, u32[]{:S(2)}, u32[]{:S(2)}) %all-to-all-start.2) | async-done | bytes 2228256 | tf_op jit(solution)/shard_map/all_to_all | solution.py:315
  222.0 6.2 %shard_map.84 = (f32[16,64,128]{2,1,0:T(8,128)S(1)}, f32[16,64,128]{2,1,0:T(8,128)S(1)}) custom-call(s32[128]{0:T(128)S(1)} %get-tuple-element.20.slot_ref, bf16[16,64,128]{2,1,0:T(8,128)(2,1)S(1)} %bitcast.16, bf16[16,2,8,128]{3,2,1,0:T(8,128)(2,1)S(1)} %bitcast.17, bf16[64,136,128]{2,1,0:T(8,128)(2,1)S(1)} %all-to-all-done.2.served_ref), custom_call_target="tpu_custom_call" | custom-call | tf_op jit(solution)/shard_map/pallas_call | solution.py:238
  228.1 0.0 copy-start.1
  228.1 0.8 copy-done.1
  228.9 0.0 copy-start.2
  228.9 0.8 copy-done.2
  229.7 54.1 %all-gather.2.cloned.1.call-done = bf16[64,128,128]{2,1,0:T(8,128)(2,1)} async-done(((bf16[1,128,128]{2,1,0:T(8,128)(2,1)}), bf16[64,128,128]{2,1,0:T(8,128)(2,1)}) %all-gather.2.cloned.1.call-update) | async-done | bytes 2097168 | tf_op jit(solution)/shard_map/all_gather | solution.py:333
  283.8 24.5 %shard_map.85 = bf16[16,64,128]{2,1,0:T(8,128)(2,1)} custom-call(bf16[16,64,128]{2,1,0:T(8,128)(2,1)} %bitcast.14, f32[16,64,128]{2,1,0:T(8,128)} %copy-done.1, f32[16,64,128]{2,1,0:T(8,128)} %copy-done.2, bf16[8,4,2,128,128]{4,3,2,1,0:T(8,128)(2,1)} %bitcast.20), custom_call_target="tpu_custom_call" | custom-call | tf_op jit(solution)/shard_map/pallas_call | solution.py:301
  (2 shorter events, 0.0 us)
Async XLA Ops:
  6.5 0.7 copy-start.3
  10.9 16.8 %copy-start.7 = (s32[16,8]{0,1:T(8,128)S(1)}, s32[16,8]{0,1:T(8,128)}, u32[]{:S(2)}) copy-start(s32[16,8]{0,1:T(8,128)} %param.14) | copy-start | bytes 1540
  10.9 16.9 %copy-start.8 = (s32[16,8]{0,1:T(8,128)S(1)}, s32[16,8]{0,1:T(8,128)}, u32[]{:S(2)}) copy-start(s32[16,8]{0,1:T(8,128)} %param.15) | copy-start | bytes 1540
  10.9 17.6 %copy-start = (bf16[16,8,8,128]{3,2,1,0:T(8,128)(2,1)S(1)}, bf16[16,8,8,128]{3,2,1,0:T(8,128)(2,1)}, u32[]{:S(2)}) copy-start(bf16[16,8,8,128]{3,2,1,0:T(8,128)(2,1)} %param.10) | copy-start | bytes 786436
  10.9 17.6 %copy-start.4 = (s32[16]{0:T(128)S(1)}, s32[16]{0:T(128)}, u32[]{:S(2)}) copy-start(s32[16]{0:T(128)} %len_ref.1) | copy-start | bytes 196
  10.9 68.7 %all-to-all-start.1 = ((bf16[64,128,128]{2,1,0:T(8,128)(2,1)}), bf16[64,128,128]{2,1,0:T(8,128)(2,1)S(1)}, u32[]{:S(2)}, u32[]{:S(2)}) async-start(bf16[64,128,128]{2,1,0:T(8,128)(2,1)} %shard_map.83), calls=%async_computation.1 | async-start | bytes 4194304 | tf_op jit(solution)/shard_map/all_to_all | solution.py:315
  79.6 1.4 copy-start.5
  159.3 10.0 %copy-start.6 = (bf16[16,8,1,2,128]{4,3,2,1,0:T(2,128)(2,1)S(1)}, bf16[16,8,1,2,128]{4,3,2,1,0:T(2,128)(2,1)}, u32[]{:S(2)}) copy-start(bf16[16,8,1,2,128]{4,3,2,1,0:T(2,128)(2,1)} %param.11) | copy-start | bytes 196612
  159.3 62.7 %all-to-all-start.2 = ((bf16[64,136,128]{2,1,0:T(8,128)(2,1)}), bf16[64,136,128]{2,1,0:T(8,128)(2,1)S(1)}, u32[]{:S(2)}, u32[]{:S(2)}) async-start(bf16[64,136,128]{2,1,0:T(8,128)(2,1)} %get-tuple-element.26), calls=%async_computation.2 | async-start | bytes 4456448 | tf_op jit(solution)/shard_map/all_to_all | solution.py:315
  167.8 116.0 %all-gather.2.cloned.1.call-start = ((), (), s32[]{:S(2)}) async-start(), calls=%async_computation.3 | async-start | bytes 2129920 | tf_op jit(solution)/shard_map/all_gather | solution.py:333
  228.1 0.8 copy-start.1
  228.9 0.8 copy-start.2
Sparse Core Ops, SparseCore 0:
  171.7 112.0 all-gather.1

commit v6 on v5

--- a/solution.py
+++ b/solution.py
@@ -13,7 +13,6 @@
 EXTRA = 8
 MERGE_BLOCK = 2
 VMEM_LIMIT = 48 * 1024 * 1024
-HOT_VMEM_LIMIT = 56 * 1024 * 1024
 
 SMEM_SPEC = pl.BlockSpec(memory_space=pltpu.SMEM)
 HBM_SPEC = pl.BlockSpec(memory_space=pltpu.HBM)
@@ -248,33 +247,22 @@
     )(slots, q, fresh, served)
 
 
-def hot_kernel(q_ref, mix_ref, stat_ref, hot_ref, out_ref, kv_ref, sems, *, factor, block):
+def hot_kernel(q_ref, mix_ref, stat_ref, hot_ref, out_ref, *, factor, block):
     chunks, per_chunk, _, page_len, lanes = hot_ref.shape
-    copies = [
-        [
-            pltpu.make_async_copy(hot_ref.at[c, :, part], kv_ref.at[c, part], sems.at[c, part])
-            for part in range(2)
-        ]
-        for c in range(chunks)
-    ]
-    for pair in copies:
-        for copy in pair:
-            copy.start()
     requests, rows, _ = q_ref.shape
-    for n in range(requests // block):
-        at = slice(n * block, (n + 1) * block)
+
+    def one(n, carry):
+        at = pl.ds(n * block, block)
         q = q_ref[at].reshape(block * rows, lanes)
         stat = stat_ref[at].reshape(block * rows, lanes)
-        top = stat[:, 0:1]
-        total = stat[:, 1:2]
+        lane = lax.broadcasted_iota(jnp.int32, stat.shape, 1)
+        top = jnp.max(jnp.where(lane == 0, stat, 2 * NEG_FILL), axis=1, keepdims=True)
+        total = jnp.sum(jnp.where(lane == 1, stat, 0.0), axis=1, keepdims=True)
         mix = mix_ref[at].reshape(block * rows, lanes)
         for c in range(chunks):
-            if n == 0:
-                for copy in copies[c]:
-                    copy.wait()
             sc = lax.dot_general(
                 q,
-                kv_ref[c, 0].reshape(per_chunk * page_len, lanes),
+                hot_ref[c, :, 0].reshape(per_chunk * page_len, lanes),
                 (((1,), (1,)), ((), ())),
                 preferred_element_type=jnp.float32,
             )
@@ -284,11 +272,14 @@
             total = total * keep + jnp.sum(ex, axis=1, keepdims=True)
             mix = mix * keep + jnp.dot(
                 ex.astype(jnp.bfloat16),
-                kv_ref[c, 1].reshape(per_chunk * page_len, lanes),
+                hot_ref[c, :, 1].reshape(per_chunk * page_len, lanes),
                 preferred_element_type=jnp.float32,
             )
             top = new_top
         out_ref[at] = (mix / total).astype(out_ref.dtype).reshape(block, rows, lanes)
+        return carry
+
+    lax.fori_loop(0, requests // block, one, 0)
 
 
 def attend_hot(q, mix, stat, hot, factor):
@@ -301,13 +292,9 @@
     return pl.pallas_call(
         functools.partial(hot_kernel, factor=factor, block=block),
         out_shape=jax.ShapeDtypeStruct(q.shape, q.dtype),
-        in_specs=[VMEM_SPEC] * 3 + [HBM_SPEC],
+        in_specs=[VMEM_SPEC] * 4,
         out_specs=VMEM_SPEC,
-        scratch_shapes=[
-            pltpu.VMEM((chunks, 2, pages // chunks, page_len, lanes), hot.dtype),
-            pltpu.SemaphoreType.DMA((chunks, 2)),
-        ],
-        compiler_params=pltpu.CompilerParams(vmem_limit_bytes=HOT_VMEM_LIMIT),
+        compiler_params=pltpu.CompilerParams(vmem_limit_bytes=VMEM_LIMIT),
     )(q, mix, stat, hot)
 
 
@@ -330,19 +317,19 @@
     asked, slots = ask(context_len, page_holder, page_index, q, groups, page_pool.shape[3])
     asked, dealt = lax.optimization_barrier((asked, dealt))
     share = lax.dynamic_index_in_dim(dealt, hot_owner[0], 0, keepdims=False)
+    asked, share = lax.optimization_barrier((asked, share))
     hot = lax.all_gather(share, "group", axis=0, tiled=False)
 
-    def attend(sent, pages):
+    def attend(sent, pages, slots, q, fresh):
         sent = exchange(sent)
         table = sent[:, body : body + CAP, 0:2].astype(jnp.int32).reshape(-1)
-        return serve(table, sent, pages, factor)
-
-    def nothing(sent, pages):
-        return jnp.zeros_like(sent)
-
-    served = lax.cond(hot_owner[0] >= 0, attend, nothing, asked, pool)
-    served = exchange(served)
-    mix, stat = merge(slots, q, fresh, served, factor, local_heads, max_pages)
+        served = exchange(serve(table, sent, pages, factor))
+        return merge(slots, q, fresh, served, factor, local_heads, max_pages)
+
+    def nothing(sent, pages, slots, q, fresh):
+        return (jnp.zeros(q.shape, jnp.float32),) * 2
+
+    mix, stat = lax.cond(hot_owner[0] >= 0, attend, nothing, asked, pool, slots, q, fresh)
     attended = attend_hot(q, mix, stat, hot, factor)
     return attended.reshape(requests, steps, local_heads, head_dim)
 

time: 316 us -> 256 us (0.81)
  waiting for transfers between devices: 151 us -> 50.2 us
  blocking collectives: 68 us -> 138 us
  Pallas kernels: 51.1 us -> 32.7 us
  starting transfers between devices: 25.3 us -> 16.8 us
    all_to_all x1 -> x2, blocking collectives: 68 us -> 138 us  [exchange(): lax.all_to_all(value, 'group', split_axis=0, concat_axis=0, tiled=True)]
    all_to_all x2 -> x1, waiting for transfers between devices: 97.2 us -> 44.4 us  [exchange(): lax.all_to_all(value, 'group', split_axis=0, concat_axis=0, tiled=True)]
    all_gather x1, waiting for transfers between devices: 54.1 us -> 5.75 us  [on_device(): hot = lax.all_gather(share, 'group', axis=0, tiled=False)]
    pallas_call x1, Pallas kernels: 24.5 us -> 7.64 us  [attend_hot(): pl.pallas_call(functools.partial(hot_kernel, factor=factor, block=block),...]
    all_to_all x2 -> x1, starting transfers between devices: 25.2 us -> 16.7 us  [exchange(): lax.all_to_all(value, 'group', split_axis=0, concat_axis=0, tiled=True)]
  transfers between devices with their start and end apart: 3 -> 2, of which waited for: 3 -> 2; matrix products, arithmetic and copies ran while one was open for 0% -> 0% of each run, Pallas kernels for 4% -> 8%
where the time goes in v6:
time: 256 us; the launch traced here: 255 us
  blocking collectives  138 us (54%)
  waiting for transfers between devices  50.2 us (20%)
  Pallas kernels  32.7 us (13%)
  starting transfers between devices  16.8 us (7%)
  between operations  14.2 us (6%)
  local copies, waits for them, and re-layouts  3.19 us (1%)
    all_to_all x2, blocking collectives, exchange(): lax.all_to_all(value, 'group', split_axis=0, concat_axis=0, tiled=True)  138 us
    all_to_all x1, waiting for transfers between devices, exchange(): lax.all_to_all(value, 'group', split_axis=0, concat_axis=0, tiled=True)  44.4 us
    all_to_all x1, starting transfers between devices, exchange(): lax.all_to_all(value, 'group', split_axis=0, concat_axis=0, tiled=True)  16.7 us
    pallas_call x1, Pallas kernels, serve(): pl.pallas_call(functools.partial(serve_kernel, factor=factor, block=block...  8.76 us
    pallas_call x1, Pallas kernels, attend_hot(): pl.pallas_call(functools.partial(hot_kernel, factor=factor, block=block),...  7.64 us
    pallas_call x1, Pallas kernels, ask(): pl.pallas_call(functools.partial(ask_kernel, page_len=page_len), out_shap...  6.65 us
    pallas_call x1, Pallas kernels, merge(): pl.pallas_call(functools.partial(merge_kernel, factor=factor, per_kv=per_...  5.97 us
    all_gather x1, waiting for transfers between devices, on_device(): hot = lax.all_gather(share, 'group', axis=0, tiled=False)  5.75 us
  transfers between devices with their start and end apart: 2, of which 2 were waited for; matrix products, arithmetic and copies ran while one was open for 0% of the time, Pallas kernels for 8%

profile of v6, /device:TPU:6, one launch (start us, length us, event | category | flops | bytes accessed | tf_op | source)
XLA Modules:
  0.0 255.5 jit_solution(3936789193860603240)
XLA Ops:
  6.5 0.0 copy-start.1
  6.5 0.7 copy-done.1
  7.2 3.7 %shard_map.83 = bf16[64,128,128]{2,1,0:T(8,128)(2,1)} custom-call(s32[32]{0:T(128)S(1)} %copy-done.1, bf16[64,2,128,128]{3,2,1,0:T(8,128)(2,1)} %bitcast.17), custom_call_target="tpu_custom_call" | custom-call | tf_op jit(solution)/shard_map/pallas_call | solution.py:37
  10.9 0.0 copy-start.5
  10.9 0.0 copy-start.6
  10.9 0.0 copy-start.2
  10.9 0.0 copy-start.3
  10.9 0.0 copy-start.4
  10.9 16.7 %all-to-all-start.2 = ((bf16[64,128,128]{2,1,0:T(8,128)(2,1)}), bf16[64,128,128]{2,1,0:T(8,128)(2,1)S(1)}, u32[]{:S(2)}, u32[]{:S(2)}) async-start(bf16[64,128,128]{2,1,0:T(8,128)(2,1)} %shard_map.83), calls=%async_computation.2 | async-start | bytes 4194304 | tf_op jit(solution)/shard_map/all_to_all | solution.py:302
  27.7 0.0 all-gather.3.cloned.1.call-start
  28.4 0.0 copy-done.5
  28.4 0.1 copy.12.holder_ref
  28.5 0.0 copy-done.6
  28.5 0.1 copy.13.index_ref
  28.5 0.0 copy-done.2
  28.5 0.0 copy-done.3
  28.5 6.7 %shard_map.82 = (bf16[64,136,128]{2,1,0:T(8,128)(2,1)}, s32[128]{0:T(128)S(1)}) custom-call(s32[16]{0:T(128)S(1)} %copy-done.2, s32[16,8]{1,0:T(8,128)S(1)} %copy.12.holder_ref, s32[16,8]{1,0:T(8,128)S(1)} %copy.13.index_ref, bf16[16,64,128]{2,1,0:T(8,128)(2,1)S(1)} %bitcast.19), custom_call_target="tpu_custom_call" | custom-call | tf_op jit(solution)/shard_map/pallas_call | solution.py:91
  35.2 44.4 %all-to-all-done.2 = bf16[64,128,128]{2,1,0:T(8,128)(2,1)S(1)} async-done(((bf16[64,128,128]{2,1,0:T(8,128)(2,1)}), bf16[64,128,128]{2,1,0:T(8,128)(2,1)S(1)}, u32[]{:S(2)}, u32[]{:S(2)}) %all-to-all-start.2) | async-done | bytes 2097184 | tf_op jit(solution)/shard_map/all_to_all | solution.py:302
  79.6 0.6 dynamic-slice_bitcast_fusion
  80.2 0.0 all-gather.3.cloned.1.call-update
  80.3 0.0 copy-done.4
  80.3 153.3 %conditional.1 = ((f32[16,64,128]{2,1,0:T(8,128)S(1)}, f32[16,64,128]{2,1,0:T(8,128)S(1)})) conditional(s32[]{:T(128)} %convert_element_type.4, () %tuple.14, (bf16[64,136,128]{2,1,0:T(8,128)(2,1)}, bf16[64,2,128,128]{3,2,1,0:T(8,128)(2,1)}, s32[128]{0:T(128)S(1)}, bf16[16,64,128]{2,1,0:T(8,128)(2,1)S(1)}, bf16[16,2,8,128]{3,2,1,0:T(8,128)(2,1)S(1)}) %tuple.26), branch_computations={%region_0.1_spmd, %region_1.2_spmd} | conditional | flops 256 | bytes 8916488 | solution.py:332
  80.3 67.7 %all_to_all.13.asked_ref = bf16[64,136,128]{2,1,0:T(8,128)(2,1)S(1)} all-to-all(bf16[64,136,128]{2,1,0:T(8,128)(2,1)} %get-tuple-element.18), channel_id=1, replica_groups=mesh['group'=64,'head'=8] {'group'}, dimensions={0} | all-to-all | bytes 4456448 | tf_op jit(solution)/shard_map/cond/branch_1_fun/all_to_all | solution.py:302
  148.0 0.1 reshape.18.table_ref
  148.2 8.8 %branch_1_fun.2 = bf16[64,136,128]{2,1,0:T(8,128)(2,1)S(1)} custom-call(s32[256]{0:T(256)S(1)} %reshape.18.table_ref, bf16[64,136,128]{2,1,0:T(8,128)(2,1)S(1)} %all_to_all.13.asked_ref, bf16[64,2,128,128]{3,2,1,0:T(8,128)(2,1)} %get-tuple-element.19.pool_ref), custom_call_target="tpu_custom_call" | custom-call | tf_op jit(solution)/shard_map/cond/branch_1_fun/pallas_call | solution.py:159
  156.9 70.7 %all_to_all.14.served_ref = bf16[64,136,128]{2,1,0:T(8,128)(2,1)S(1)} all-to-all(bf16[64,136,128]{2,1,0:T(8,128)(2,1)S(1)} %branch_1_fun.2), channel_id=1, replica_groups=mesh['group'=64,'head'=8] {'group'}, dimensions={0} | all-to-all | bytes 4456448 | tf_op jit(solution)/shard_map/cond/branch_1_fun/all_to_all | solution.py:302
  227.7 6.0 %branch_1_fun.3 = (f32[16,64,128]{2,1,0:T(8,128)S(1)}, f32[16,64,128]{2,1,0:T(8,128)S(1)}) custom-call(s32[128]{0:T(128)S(1)} %get-tuple-element.15.slot_ref, bf16[16,64,128]{2,1,0:T(8,128)(2,1)S(1)} %get-tuple-element.16.q_ref, bf16[16,2,8,128]{3,2,1,0:T(8,128)(2,1)S(1)} %get-tuple-element.17.fresh_ref, bf16[64,136,128]{2,1,0:T(8,128)(2,1)S(1)} %all_to_all.14.served_ref), custom_call_target="tpu_custom_call" | custom-call | tf_op jit(solution)/shard_map/cond/branch_1_fun/pallas_call | solution.py:237
  233.6 5.8 %all-gather.3.cloned.1.call-done = bf16[8192,128]{1,0:T(8,128)(2,1)} async-done(((bf16[128,128]{1,0:T(8,128)(2,1)}), bf16[8192,128]{1,0:T(8,128)(2,1)}) %all-gather.3.cloned.1.call-update) | async-done | bytes 2097168 | tf_op jit(solution)/shard_map/all_gather | solution.py:321
  239.4 0.0 copy-start
  239.4 1.6 copy-done
  241.0 7.6 %shard_map.84 = bf16[16,64,128]{2,1,0:T(8,128)(2,1)} custom-call(bf16[16,64,128]{2,1,0:T(8,128)(2,1)S(1)} %bitcast.21, f32[16,64,128]{2,1,0:T(8,128)S(1)} %get-tuple-element.33.mix_ref, f32[16,64,128]{2,1,0:T(8,128)S(1)} %get-tuple-element.34.stat_ref, bf16[8,4,2,128,128]{4,3,2,1,0:T(8,128)(2,1)S(1)} %bitcast.16), custom_call_target="tpu_custom_call" | custom-call | tf_op jit(solution)/shard_map/pallas_call | solution.py:292
  (2 shorter events, 0.0 us)
Async XLA Ops:
  6.5 0.7 copy-start.1
  10.9 17.5 %copy-start.5 = (s32[16,8]{0,1:T(8,128)S(1)}, s32[16,8]{0,1:T(8,128)}, u32[]{:S(2)}) copy-start(s32[16,8]{0,1:T(8,128)} %param.14) | copy-start | bytes 1540
  10.9 17.6 %copy-start.6 = (s32[16,8]{0,1:T(8,128)S(1)}, s32[16,8]{0,1:T(8,128)}, u32[]{:S(2)}) copy-start(s32[16,8]{0,1:T(8,128)} %param.15) | copy-start | bytes 1540
  10.9 17.6 %copy-start.2 = (s32[16]{0:T(128)S(1)}, s32[16]{0:T(128)}, u32[]{:S(2)}) copy-start(s32[16]{0:T(128)} %len_ref.1) | copy-start | bytes 196
  10.9 17.6 %copy-start.3 = (bf16[16,8,8,128]{3,2,1,0:T(8,128)(2,1)S(1)}, bf16[16,8,8,128]{3,2,1,0:T(8,128)(2,1)}, u32[]{:S(2)}) copy-start(bf16[16,8,8,128]{3,2,1,0:T(8,128)(2,1)} %param.10) | copy-start | bytes 786436
  10.9 69.3 %copy-start.4 = (bf16[16,8,1,2,128]{4,3,2,1,0:T(2,128)(2,1)S(1)}, bf16[16,8,1,2,128]{4,3,2,1,0:T(2,128)(2,1)}, u32[]{:S(2)}) copy-start(bf16[16,8,1,2,128]{4,3,2,1,0:T(2,128)(2,1)} %param.11) | copy-start | bytes 196612
  10.9 68.7 %all-to-all-start.2 = ((bf16[64,128,128]{2,1,0:T(8,128)(2,1)}), bf16[64,128,128]{2,1,0:T(8,128)(2,1)S(1)}, u32[]{:S(2)}, u32[]{:S(2)}) async-start(bf16[64,128,128]{2,1,0:T(8,128)(2,1)} %shard_map.83), calls=%async_computation.2 | async-start | bytes 4194304 | tf_op jit(solution)/shard_map/all_to_all | solution.py:302
  27.7 211.7 %all-gather.3.cloned.1.call-start = ((), (), s32[]{:S(2)}) async-start(), calls=%async_computation.3 | async-start | bytes 2129920 | tf_op jit(solution)/shard_map/all_gather | solution.py:321
  239.4 1.6 copy-start
Sparse Core Ops, SparseCore 0:
  80.4 158.9 all-gather.2

commit v7 on v6

--- a/solution.py
+++ b/solution.py
@@ -286,8 +286,8 @@
     requests, rows, lanes = q.shape
     pages = hot.shape[0] // 2
     page_len = hot.shape[1]
-    block = math.gcd(requests, 8)
-    chunks = math.gcd(pages, 8)
+    block = math.gcd(requests, 16)
+    chunks = math.gcd(pages, 4)
     hot = hot.reshape(chunks, pages // chunks, 2, page_len, lanes)
     return pl.pallas_call(
         functools.partial(hot_kernel, factor=factor, block=block),

time: 256 us -> 255 us (level)
  no operation moved by 1% of the time
where the time goes in v7:
time: 255 us; the launch traced here: 254 us
  blocking collectives  138 us (54%)
  waiting for transfers between devices  50.4 us (20%)
  Pallas kernels  31.4 us (12%)
  starting transfers between devices  16.8 us (7%)
  between operations  14.2 us (6%)
  local copies, waits for them, and re-layouts  3.19 us (1%)
    all_to_all x2, blocking collectives, exchange(): lax.all_to_all(value, 'group', split_axis=0, concat_axis=0, tiled=True)  138 us
    all_to_all x1, waiting for transfers between devices, exchange(): lax.all_to_all(value, 'group', split_axis=0, concat_axis=0, tiled=True)  44.6 us
    all_to_all x1, starting transfers between devices, exchange(): lax.all_to_all(value, 'group', split_axis=0, concat_axis=0, tiled=True)  16.7 us
    pallas_call x1, Pallas kernels, serve(): pl.pallas_call(functools.partial(serve_kernel, factor=factor, block=block...  8.76 us
    pallas_call x1, Pallas kernels, attend_hot(): pl.pallas_call(functools.partial(hot_kernel, factor=factor, block=block),...  6.54 us
    pallas_call x1, Pallas kernels, ask(): pl.pallas_call(functools.partial(ask_kernel, page_len=page_len), out_shap...  6.46 us
    pallas_call x1, Pallas kernels, merge(): pl.pallas_call(functools.partial(merge_kernel, factor=factor, per_kv=per_...  5.96 us
    all_gather x1, waiting for transfers between devices, on_device(): hot = lax.all_gather(share, 'group', axis=0, tiled=False)  5.76 us
  transfers between devices with their start and end apart: 2, of which 2 were waited for; matrix products, arithmetic and copies ran while one was open for 0% of the time, Pallas kernels for 8%

profile of v7, /device:TPU:6, one launch (start us, length us, event | category | flops | bytes accessed | tf_op | source)
XLA Modules:
  0.0 254.4 jit_solution(1193089845640183782)
XLA Ops:
  6.5 0.0 copy-start.1
  6.5 0.7 copy-done.1
  7.2 3.7 %shard_map.83 = bf16[64,128,128]{2,1,0:T(8,128)(2,1)} custom-call(s32[32]{0:T(128)S(1)} %copy-done.1, bf16[64,2,128,128]{3,2,1,0:T(8,128)(2,1)} %bitcast.17), custom_call_target="tpu_custom_call" | custom-call | tf_op jit(solution)/shard_map/pallas_call | solution.py:37
  10.9 0.0 copy-start.5
  10.9 0.0 copy-start.6
  10.9 0.0 copy-start.2
  10.9 0.0 copy-start.3
  10.9 0.0 copy-start.4
  10.9 16.7 %all-to-all-start.2 = ((bf16[64,128,128]{2,1,0:T(8,128)(2,1)}), bf16[64,128,128]{2,1,0:T(8,128)(2,1)S(1)}, u32[]{:S(2)}, u32[]{:S(2)}) async-start(bf16[64,128,128]{2,1,0:T(8,128)(2,1)} %shard_map.83), calls=%async_computation.2 | async-start | bytes 4194304 | tf_op jit(solution)/shard_map/all_to_all | solution.py:302
  27.7 0.0 all-gather.3.cloned.1.call-start
  28.4 0.0 copy-done.5
  28.4 0.1 copy.12.holder_ref
  28.5 0.0 copy-done.6
  28.5 0.1 copy.13.index_ref
  28.5 0.0 copy-done.2
  28.5 0.0 copy-done.3
  28.5 6.5 %shard_map.82 = (bf16[64,136,128]{2,1,0:T(8,128)(2,1)}, s32[128]{0:T(128)S(1)}) custom-call(s32[16]{0:T(128)S(1)} %copy-done.2, s32[16,8]{1,0:T(8,128)S(1)} %copy.12.holder_ref, s32[16,8]{1,0:T(8,128)S(1)} %copy.13.index_ref, bf16[16,64,128]{2,1,0:T(8,128)(2,1)S(1)} %bitcast.19), custom_call_target="tpu_custom_call" | custom-call | tf_op jit(solution)/shard_map/pallas_call | solution.py:91
  35.0 44.6 %all-to-all-done.2 = bf16[64,128,128]{2,1,0:T(8,128)(2,1)S(1)} async-done(((bf16[64,128,128]{2,1,0:T(8,128)(2,1)}), bf16[64,128,128]{2,1,0:T(8,128)(2,1)S(1)}, u32[]{:S(2)}, u32[]{:S(2)}) %all-to-all-start.2) | async-done | bytes 2097184 | tf_op jit(solution)/shard_map/all_to_all | solution.py:302
  79.6 0.6 dynamic-slice_bitcast_fusion
  80.2 0.0 all-gather.3.cloned.1.call-update
  80.3 0.0 copy-done.4
  80.3 153.3 %conditional.1 = ((f32[16,64,128]{2,1,0:T(8,128)S(1)}, f32[16,64,128]{2,1,0:T(8,128)S(1)})) conditional(s32[]{:T(128)} %convert_element_type.4, () %tuple.14, (bf16[64,136,128]{2,1,0:T(8,128)(2,1)}, bf16[64,2,128,128]{3,2,1,0:T(8,128)(2,1)}, s32[128]{0:T(128)S(1)}, bf16[16,64,128]{2,1,0:T(8,128)(2,1)S(1)}, bf16[16,2,8,128]{3,2,1,0:T(8,128)(2,1)S(1)}) %tuple.26), branch_computations={%region_0.1_spmd, %region_1.2_spmd} | conditional | flops 256 | bytes 8916488 | solution.py:332
  80.3 67.7 %all_to_all.13.asked_ref = bf16[64,136,128]{2,1,0:T(8,128)(2,1)S(1)} all-to-all(bf16[64,136,128]{2,1,0:T(8,128)(2,1)} %get-tuple-element.18), channel_id=1, replica_groups=mesh['group'=64,'head'=8] {'group'}, dimensions={0} | all-to-all | bytes 4456448 | tf_op jit(solution)/shard_map/cond/branch_1_fun/all_to_all | solution.py:302
  148.0 0.1 reshape.18.table_ref
  148.2 8.8 %branch_1_fun.2 = bf16[64,136,128]{2,1,0:T(8,128)(2,1)S(1)} custom-call(s32[256]{0:T(256)S(1)} %reshape.18.table_ref, bf16[64,136,128]{2,1,0:T(8,128)(2,1)S(1)} %all_to_all.13.asked_ref, bf16[64,2,128,128]{3,2,1,0:T(8,128)(2,1)} %get-tuple-element.19.pool_ref), custom_call_target="tpu_custom_call" | custom-call | tf_op jit(solution)/shard_map/cond/branch_1_fun/pallas_call | solution.py:159
  156.9 70.7 %all_to_all.14.served_ref = bf16[64,136,128]{2,1,0:T(8,128)(2,1)S(1)} all-to-all(bf16[64,136,128]{2,1,0:T(8,128)(2,1)S(1)} %branch_1_fun.2), channel_id=1, replica_groups=mesh['group'=64,'head'=8] {'group'}, dimensions={0} | all-to-all | bytes 4456448 | tf_op jit(solution)/shard_map/cond/branch_1_fun/all_to_all | solution.py:302
  227.7 6.0 %branch_1_fun.3 = (f32[16,64,128]{2,1,0:T(8,128)S(1)}, f32[16,64,128]{2,1,0:T(8,128)S(1)}) custom-call(s32[128]{0:T(128)S(1)} %get-tuple-element.15.slot_ref, bf16[16,64,128]{2,1,0:T(8,128)(2,1)S(1)} %get-tuple-element.16.q_ref, bf16[16,2,8,128]{3,2,1,0:T(8,128)(2,1)S(1)} %get-tuple-element.17.fresh_ref, bf16[64,136,128]{2,1,0:T(8,128)(2,1)S(1)} %all_to_all.14.served_ref), custom_call_target="tpu_custom_call" | custom-call | tf_op jit(solution)/shard_map/cond/branch_1_fun/pallas_call | solution.py:237
  233.6 5.8 %all-gather.3.cloned.1.call-done = bf16[8192,128]{1,0:T(8,128)(2,1)} async-done(((bf16[128,128]{1,0:T(8,128)(2,1)}), bf16[8192,128]{1,0:T(8,128)(2,1)}) %all-gather.3.cloned.1.call-update) | async-done | bytes 2097168 | tf_op jit(solution)/shard_map/all_gather | solution.py:321
  239.4 0.0 copy-start
  239.4 1.6 copy-done
  241.0 6.5 %shard_map.84 = bf16[16,64,128]{2,1,0:T(8,128)(2,1)} custom-call(bf16[16,64,128]{2,1,0:T(8,128)(2,1)S(1)} %bitcast.21, f32[16,64,128]{2,1,0:T(8,128)S(1)} %get-tuple-element.33.mix_ref, f32[16,64,128]{2,1,0:T(8,128)S(1)} %get-tuple-element.34.stat_ref, bf16[4,8,2,128,128]{4,3,2,1,0:T(8,128)(2,1)S(1)} %bitcast.16), custom_call_target="tpu_custom_call" | custom-call | tf_op jit(solution)/shard_map/pallas_call | solution.py:292
  (2 shorter events, 0.0 us)
Async XLA Ops:
  6.5 0.7 copy-start.1
  10.9 17.5 %copy-start.5 = (s32[16,8]{0,1:T(8,128)S(1)}, s32[16,8]{0,1:T(8,128)}, u32[]{:S(2)}) copy-start(s32[16,8]{0,1:T(8,128)} %param.14) | copy-start | bytes 1540
  10.9 17.6 %copy-start.6 = (s32[16,8]{0,1:T(8,128)S(1)}, s32[16,8]{0,1:T(8,128)}, u32[]{:S(2)}) copy-start(s32[16,8]{0,1:T(8,128)} %param.15) | copy-start | bytes 1540
  10.9 17.6 %copy-start.2 = (s32[16]{0:T(128)S(1)}, s32[16]{0:T(128)}, u32[]{:S(2)}) copy-start(s32[16]{0:T(128)} %len_ref.1) | copy-start | bytes 196
  10.9 17.6 %copy-start.3 = (bf16[16,8,8,128]{3,2,1,0:T(8,128)(2,1)S(1)}, bf16[16,8,8,128]{3,2,1,0:T(8,128)(2,1)}, u32[]{:S(2)}) copy-start(bf16[16,8,8,128]{3,2,1,0:T(8,128)(2,1)} %param.10) | copy-start | bytes 786436
  10.9 69.3 %copy-start.4 = (bf16[16,8,1,2,128]{4,3,2,1,0:T(2,128)(2,1)S(1)}, bf16[16,8,1,2,128]{4,3,2,1,0:T(2,128)(2,1)}, u32[]{:S(2)}) copy-start(bf16[16,8,1,2,128]{4,3,2,1,0:T(2,128)(2,1)} %param.11) | copy-start | bytes 196612
  10.9 68.7 %all-to-all-start.2 = ((bf16[64,128,128]{2,1,0:T(8,128)(2,1)}), bf16[64,128,128]{2,1,0:T(8,128)(2,1)S(1)}, u32[]{:S(2)}, u32[]{:S(2)}) async-start(bf16[64,128,128]{2,1,0:T(8,128)(2,1)} %shard_map.83), calls=%async_computation.2 | async-start | bytes 4194304 | tf_op jit(solution)/shard_map/all_to_all | solution.py:302
  27.7 211.7 %all-gather.3.cloned.1.call-start = ((), (), s32[]{:S(2)}) async-start(), calls=%async_computation.3 | async-start | bytes 2129920 | tf_op jit(solution)/shard_map/all_gather | solution.py:321
  239.4 1.6 copy-start
Sparse Core Ops, SparseCore 0:
  80.4 158.9 all-gather.2
